TPU v7x, 512 devices: a whole 4x4x16 slice. The times are simulated.
512 devices in a mesh: gx: 8 (over x, core), gy: 16 (over z), gz: 4 (over y).
Axes of the slice: x: 4, y: 4, z: 16, core: 2. Of those that a mesh axis runs over, the one named last changes fastest.
Arguments:
- displacement: float32 [3, 32, 256, 512], P(None, 'gx', 'gy', 'gz'), may hold values from -6 to 6
- density: float32 [32, 256, 512], P('gx', 'gy', 'gz'), may hold values from 0.3 to 1
- solid: int32 [32, 256, 512], P('gx', 'gy', 'gz'), may hold values from 0 to 1, as said below
- material: int32 [32, 256, 512], P('gx', 'gy', 'gz'), may hold values from 0 to 3
- fixed: int32 [32, 256, 512], P('gx', 'gy', 'gz'), may hold values 0 or 1
Outputs:
- adjoint: float32 [3, 32, 256, 512], P(None, 'gx', 'gy', 'gz')
- sensitivity: float32 [32, 256, 512], P('gx', 'gy', 'gz')
Inputs may be any that keep to these rules, and one draw needn't show every extreme that they name: 1 marks a solid element, 0 a void one.
All inputs are finite; a program needn't handle non-finite values. No bound on the sum of `fixed` on one device may be relied on, other than what follows from the above.
Results may differ from a plain program's by a relative error of at most 0.0003.
Values sent between devices are 32-bit elements; how exact they have to be, the bound alone decides.
A program may use at most 64 MiB of HBM per device.

v0:
```python
import functools
import itertools

import jax
import jax.numpy as jnp
import numpy as np
from jax import lax
from jax.experimental import pallas as pl
from jax.experimental.pallas import tpu as pltpu
from jax.sharding import PartitionSpec as P

POISSON = 0.3
VOID_FLOOR = 0.001
MODULI = (1.0, 0.7, 0.45, 0.25)
MESH = pl.DeviceIdType.MESH
AXES = ("gx", "gy", "gz")

BX, BY, BZ = 4, 16, 128
W = 4
NP = BX + 2 * W
ROWS = 32
CH = 3


def lame_pair():
    first = POISSON / ((1.0 + POISSON) * (1.0 - 2.0 * POISSON))
    shear = 1.0 / (2.0 * (1.0 + POISSON))
    return (first, shear)


def corner_signs():
    return [(2 * a - 1, 2 * b - 1, 2 * c - 1) for a in (0, 1) for b in (0, 1) for c in (0, 1)]


def element_table():
    first, shear = lame_pair()
    elastic = np.zeros((6, 6))
    elastic[:3, :3] = first
    for index in range(3):
        elastic[index, index] += 2.0 * shear
        elastic[index + 3, index + 3] = shear
    point = 1.0 / np.sqrt(3.0)
    matrix = np.zeros((24, 24))
    for xi in (-point, point):
        for eta in (-point, point):
            for zeta in (-point, point):
                strain = np.zeros((6, 24))
                for index, signs in enumerate(corner_signs()):
                    sa, sb, sc = signs
                    gradx = 2.0 * sa * (1 + sb * eta) * (1 + sc * zeta) / 8.0
                    grady = 2.0 * sb * (1 + sa * xi) * (1 + sc * zeta) / 8.0
                    gradz = 2.0 * sc * (1 + sa * xi) * (1 + sb * eta) / 8.0
                    strain[0, index] = gradx
                    strain[1, 8 + index] = grady
                    strain[2, 16 + index] = gradz
                    strain[3, 8 + index] = gradz
                    strain[3, 16 + index] = grady
                    strain[4, index] = gradz
                    strain[4, 16 + index] = gradx
                    strain[5, index] = grady
                    strain[5, 8 + index] = gradx
                matrix += strain.T @ elastic @ strain / 8.0
    return matrix


def chebyshev_constants():
    rowsum = float(np.max(np.sum(np.abs(element_table()), axis=1)))
    upper = max(2.0, 8.0 * max(MODULI) * rowsum)
    lower = upper / 20.0
    theta = (upper + lower) / 2.0
    delta = (upper - lower) / 2.0
    sigma = theta / delta
    rho_zero = 1.0 / sigma
    rho_one = 1.0 / (2.0 * sigma - rho_zero)
    rho_two = 1.0 / (2.0 * sigma - rho_one)
    return (theta, delta, rho_zero, rho_one, rho_two)


HALO = [d for d in itertools.product((-1, 0, 1), repeat=3) if d != (0, 0, 0)]
HALO.sort(key=lambda d: (d[2] != 0, abs(d[0]) + abs(d[1]) + abs(d[2])))


def partners(sizes):
    nx, ny, nz = sizes

    def far(d):
        return sum(min(o % n, -o % n) for o, n in zip(d, sizes))

    plane = [(a, 0, c) for a in range(nx) for c in range(nz) if (a, c) != (0, 0)]
    ring = [(0, b, 0) for b in range(1, ny)]
    return sorted(plane, key=far, reverse=True), sorted(ring, key=far, reverse=True)


GREETED = [(4, 0, 0), (4, 0, 2), (0, 4, 0), (0, -4, 0), (0, 7, 0), (0, -7, 0)]


def lanes():
    return lax.broadcasted_iota(jnp.int32, (2, 8, 128), 2)


def swapped(x):
    return jnp.stack([x[1], x[0]])


def z_next(x):
    r = pltpu.roll(x, 127, 2)
    return jnp.where(lanes() == 127, swapped(r), r)


def z_prev(x):
    r = pltpu.roll(x, 1, 2)
    return jnp.where(lanes() == 0, swapped(r), r)


def y_transform(ref, comp, plane, t):
    a = ref[comp, plane, :, 8 * t : 8 * t + 8, :]
    b = ref[comp, plane, :, 8 * t + 1 : 8 * t + 9, :]
    return a + b, b - a


def full_transform(ref, comp, plane, t):
    s, d = y_transform(ref, comp, plane, t)
    sn, dn = z_next(s), z_next(d)
    return [s + sn, sn - s, d + dn, dn - d]


def central_transform(ref, comp, plane, t):
    s, d = y_transform(ref, comp, plane, t)
    sn, dn = z_next(s), z_next(d)
    return [s + sn, sn - s, d + dn]


def central_gradients(old, new):
    return [new[0] - old[0], old[2] + new[2], old[1] + new[1]]


def stress_of(grads):
    first, shear = lame_pair()
    exx, eyy, ezz = grads[0][0], grads[1][1], grads[2][2]
    base = first * (exx + eyy + ezz)
    sxx, syy, szz = base + 2.0 * shear * exx, base + 2.0 * shear * eyy, base + 2.0 * shear * ezz
    syz = shear * (grads[1][2] + grads[2][1])
    sxz = shear * (grads[0][2] + grads[2][0])
    sxy = shear * (grads[0][1] + grads[1][0])
    return sxx, syy, szz, syz, sxz, sxy


def unit_of(s):
    sxx, syy, szz, syz, sxz, sxy = s
    return (
        sxx * sxx + syy * syy + szz * szz - sxx * syy - syy * szz - szz * sxx
        + 3.0 * (syz * syz + sxz * sxz + sxy * sxy)
    )


def element_modes(old, new):
    ss, sd, ds, dd = zip(old, new)
    return {
        "DSS": ss[1] - ss[0], "SSD": sd[0] + sd[1], "DSD": sd[1] - sd[0], "SDS": ds[0] + ds[1],
        "DDS": ds[1] - ds[0], "SDD": dd[0] + dd[1], "DDD": dd[1] - dd[0],
    }


def element_forces(modes):
    first, shear = lame_pair()
    u, v, w = modes
    s = stress_of([[m["DSS"], m["SDS"], m["SSD"]] for m in (u, v, w)])
    sxx, syy, szz, syz, sxz, sxy = [x * (1.0 / 16.0) for x in s]
    own, cross = (first + 3.0 * shear) / 48.0, first / 48.0
    twist, cube = shear / 48.0, (first + 4.0 * shear) / 144.0

    def pair(a, b):
        return own * a + cross * b, cross * a + own * b

    u_xy, w_yz = pair(u["DDS"], w["SDD"])
    u_xz, v_yz = pair(u["DSD"], v["SDD"])
    v_xy, w_xz = pair(v["DDS"], w["DSD"])
    every = u["SDD"] + v["DSD"] + w["DDS"]
    return [
        {"DSS": sxx, "SDS": sxy, "SSD": sxz, "DDS": u_xy, "DSD": u_xz,
         "SDD": twist * (every + u["SDD"]), "DDD": cube * u["DDD"]},
        {"DSS": sxy, "SDS": syy, "SSD": syz, "DDS": v_xy, "SDD": v_yz,
         "DSD": twist * (every + v["DSD"]), "DDD": cube * v["DDD"]},
        {"DSS": sxz, "SDS": syz, "SSD": szz, "SDD": w_yz, "DSD": w_xz,
         "DDS": twist * (every + w["DDS"]), "DDD": cube * w["DDD"]},
    ]


def y_gather(value, kept):
    r = pltpu.roll(value, 1, 1)
    if kept is None:
        return r, r
    rows = lax.broadcasted_iota(jnp.int32, (2, 8, 128), 1)
    return jnp.where(rows == 0, kept, r), r


def kernel(sizes, disp_in, dens_in, solid_in, mat_in, fixed_in, adj_out, sens_out,
           disp_v, dens_v, solid_v, mat_v, fixed_v, own, ylow, yhigh, zlow, zhigh, zlow_y, zhigh_y,
           rx, ry, rz, ryz, fld, mod_e, grow, lead, rhs, v0, fv0, v1, fv1, adj, sens, carry_t, carry_p,
           src1, land1, src2, land2, in_sem, send_sem, recv_sem, s1, r1, s2, r2):
    position = [lax.axis_index(a) for a in AXES]

    def at(d):
        return tuple(lax.rem(p + (o % n), n) if o % n else p for p, o, n in zip(position, d, sizes))

    plane, ring = partners(sizes)
    theta, delta, rho_zero, rho_one, rho_two = chebyshev_constants()

    loads = [
        pltpu.make_async_copy(src, dst, in_sem.at[n])
        for n, (src, dst) in enumerate(
            ((disp_in, disp_v), (dens_in, dens_v), (solid_in, solid_v), (mat_in, mat_v), (fixed_in, fixed_v))
        )
    ]
    for copy in loads:
        copy.start()
    barrier = pltpu.get_barrier_semaphore()
    greeted = HALO + GREETED
    for d in greeted:
        pl.semaphore_signal(barrier, inc=1, device_id=at(d), device_id_type=MESH)

    zero = jnp.zeros((2, 8, 128), jnp.float32)

    def clear(p, _):
        for f in range(6):
            fld[f, p, :, 24:32, :] = zero
        for c in range(3):
            fv0[c, p, :, 24:32, :] = zero
            fv1[c, p, :, 24:32, :] = zero
            adj[c, p, :, 24:32, :] = zero
        return 0

    lax.fori_loop(0, NP, clear, 0)
    for copy in loads:
        copy.wait()

    free = 1.0 - fixed_v[...].astype(jnp.float32)
    own[4] = free
    own[3] = dens_v[...]
    for c in range(3):
        own[c] = disp_v[c] * free
    material = mat_v[...]
    scale_class = jnp.zeros(material.shape, jnp.float32)
    for index in range(4):
        scale_class = scale_class + jnp.where(material == index, MODULI[index], 0.0).astype(jnp.float32)
    own[5] = scale_class * (VOID_FLOOR + (1.0 - VOID_FLOOR) * solid_v[...].astype(jnp.float32))

    lane16 = lax.broadcasted_iota(jnp.int32, (16, 128), 1)
    low = jnp.zeros((16, 128), jnp.float32)
    high = jnp.zeros((16, 128), jnp.float32)
    for f in range(6):
        for p in range(BX):
            group = 4 * (BX * f + p)
            block = own[f, p]
            mine = (lane16 >= group) & (lane16 < group + 4)
            low = jnp.where(mine, pltpu.roll(block, group, 1) if group else block, low)
            high = jnp.where(mine, pltpu.roll(block, group + 4, 1), high)
            half = 4 * (p % 2)
            ylow[f, p // 2, half : half + 4, :] = block[0:4]
            yhigh[f, p // 2, half : half + 4, :] = block[12:16]
    zlow[...] = low
    zhigh[...] = high
    for ref, value in ((zlow_y, low), (zhigh_y, high)):
        ref[0:4, :] = value[0:4]
        ref[4:8, :] = value[12:16]

    pl.semaphore_wait(barrier, len(greeted))
    halos = []
    for n, (dx, dy, dz) in enumerate(HALO):
        sx, sy, sz = 1 - dx, (1 - dy) // 2, (1 - dz) // 2
        if dz == 0 and dy == 0:
            src, dst = own, rx.at[sx // 2]
        elif dz == 0:
            src, dst = (yhigh if dy > 0 else ylow), ry.at[sx, sy]
        elif dy == 0:
            src, dst = (zhigh if dz > 0 else zlow), rz.at[sx, sz]
        else:
            src, dst = (zhigh_y if dz > 0 else zlow_y), ryz.at[sx, sy, sz]
        copy = pltpu.make_async_remote_copy(
            src_ref=src, dst_ref=dst, send_sem=send_sem.at[n], recv_sem=recv_sem.at[n],
            device_id=at((dx, dy, dz)), device_id_type=MESH,
        )
        copy.start()
        halos.append(copy)
    for copy in halos:
        copy.wait_recv()

    def inside(axis, o):
        if o == 0:
            return 1.0
        edge = 0 if o < 0 else sizes[axis] - 1
        return jnp.where(position[axis] == edge, 0.0, 1.0).astype(jnp.float32)

    half_lanes16 = lane16 < 64
    half_lanes8 = lax.broadcasted_iota(jnp.int32, (8, 128), 1) < 64

    def unpack(f, _):
        for sx in range(3):
            fx = inside(0, sx - 1)
            for p in range(BX):
                q = BX * sx + p
                block = own[f, p] if sx == 1 else rx[sx // 2, f, p] * fx
                fld[f, q, 0, 4:20, :] = block
                half = 4 * (p % 2)
                for sy, rows in ((0, 0), (1, 20)):
                    part = ry[sx, sy, f, p // 2, half : half + 4, :]
                    fld[f, q, 0, rows : rows + 4, :] = part * (fx * inside(1, 2 * sy - 1))
                group = 4 * (BX * f + p)
                below, above = rz[sx, 0] * (fx * inside(2, -1)), rz[sx, 1] * (fx * inside(2, 1))
                to_low, to_high = lax.rem(256 - group, 128), lax.rem(256 - 4 - group, 128)
                fld[f, q, 1, 4:20, :] = jnp.where(
                    half_lanes16, pltpu.roll(above, to_low, 1), pltpu.roll(below, to_high, 1)
                )
                for sy, rows in ((0, 0), (1, 20)):
                    fxy = fx * inside(1, 2 * sy - 1)
                    below, above = ryz[sx, sy, 0] * (fxy * inside(2, -1)), ryz[sx, sy, 1] * (fxy * inside(2, 1))
                    edge = jnp.where(half_lanes8, pltpu.roll(above, to_low, 1), pltpu.roll(below, to_high, 1))
                    fld[f, q, 1, rows : rows + 4, :] = edge[4:8] if sy == 0 else edge[0:4]
        return 0

    lax.fori_loop(0, 6, unpack, 0)

    def own_total(e, acc):
        for start in (4, 12):
            sides = []
            for side in range(2):
                parts = []
                for c in range(4):
                    a = fld[c, e + side, :, start : start + 8, :]
                    b = fld[c, e + side, :, start + 1 : start + 9, :]
                    s, d = a + b, b - a
                    sn, dn = z_next(s), z_next(d)
                    parts.append([(s + sn)[0], (sn - s)[0], (d + dn)[0]])
                sides.append(parts)
            old, new = sides
            grads = [[0.25 * g for g in central_gradients(old[c], new[c])] for c in range(3)]
            rho = (old[3][0] + new[3][0]) * 0.125
            modulus = rho * rho * rho * fld[5, e, 0, start : start + 8, :]
            q = modulus * modulus * unit_of(stress_of(grads))
            q = q * q
            acc = acc + q * q
        return acc

    partial = lax.fori_loop(W, W + BX, own_total, jnp.zeros((8, 128), jnp.float32))
    src1[...] = partial
    sums1 = []
    for n, d in enumerate(plane):
        copy = pltpu.make_async_remote_copy(
            src_ref=src1, dst_ref=land1.at[n], send_sem=s1.at[n], recv_sem=r1.at[n],
            device_id=at(d), device_id_type=MESH,
        )
        copy.start()
        sums1.append(copy)

    kinds = ("SS", "SD", "DS", "DD")

    def scatter(t, forces, kept, names):
        result, keep = [], []
        for c in range(3):
            by = {}
            for i, k in enumerate(kinds):
                s, d = forces[c].get("S" + k), forces[c].get("D" + k)
                if s is None and d is None:
                    continue
                if s is None:
                    lower, upper = -d, d
                elif d is None:
                    lower, upper = s, s
                else:
                    lower, upper = s - d, s + d
                by[k] = lower + carry_p[t, 4 * c + i]
                carry_p[t, 4 * c + i] = upper
            rows = []
            for k in ("S", "D"):
                s, d = by[k + "S"], by.get(k + "D")
                if d is None:
                    rows.append(s + z_prev(s))
                else:
                    rows.append((s - d) + z_prev(s + d))
            down, r = y_gather(rows[0] + rows[1], None if kept is None else kept[c])
            result.append((rows[0] - rows[1]) + down)
            keep.append(r)
        return result, keep

    def clear_carry():
        def body(i, _):
            for t in range(CH):
                carry_p[t, i] = zero
            return 0
        lax.fori_loop(0, 12, body, 0)

    def chunk(t):
        return slice(8 * t, 8 * t + 8)

    clear_carry()
    for t in range(CH):
        for c in range(4):
            for i, value in enumerate(central_transform(fld, c, 0, t)):
                carry_t[t, 4 * c + i] = value

    def stage_one(e, _):
        kept = None
        first, shear = lame_pair()
        for t in range(CH):
            grads = []
            for c in range(3):
                new = central_transform(fld, c, e + 1, t)
                old = [carry_t[t, 4 * c + i] for i in range(3)]
                for i, value in enumerate(new):
                    carry_t[t, 4 * c + i] = value
                grads.append([0.25 * g for g in central_gradients(old, new)])
            s, _d = y_transform(fld, 3, e + 1, t)
            mass = s + z_next(s)
            rho = (carry_t[t, 12] + mass) * 0.125
            carry_t[t, 12] = mass
            stiff = fld[5, e, :, chunk(t), :]
            rho_stiff = rho * rho * stiff
            modulus = rho_stiff * rho
            growth = 3.0 * rho_stiff
            mod_e[e, :, chunk(t), :] = modulus
            grow[e, :, chunk(t), :] = growth
            stress = stress_of(grads)
            unit = unit_of(stress)
            square = modulus * modulus
            q = square * unit
            q3 = q * q * q
            lead[e, :, chunk(t), :] = growth * (8.0 * q3 * modulus * unit)
            sxx, syy, szz, syz, sxz, sxy = stress
            weight = q3 * square
            tr = sxx + syy + szz
            hxx, hyy, hzz = 3.0 * sxx - tr, 3.0 * syy - tr, 3.0 * szz - tr
            base = first * (hxx + hyy + hzz)
            wxx = weight * (base + 2.0 * shear * hxx)
            wyy = weight * (base + 2.0 * shear * hyy)
            wzz = weight * (base + 2.0 * shear * hzz)
            skew = weight * (6.0 * shear)
            wyz, wxz, wxy = skew * syz, skew * sxz, skew * sxy
            forces = [
                {"DSS": wxx, "SDS": wxy, "SSD": wxz},
                {"DSS": wxy, "SDS": wyy, "SSD": wyz},
                {"DSS": wxz, "SDS": wyz, "SSD": wzz},
            ]
            load, kept = scatter(t, forces, kept, None)
            free = fld[4, e, :, chunk(t), :]
            for c in range(3):
                r = free * load[c]
                d = r * (1.0 / theta)
                rhs[c, e, :, chunk(t), :] = r
                v0[c, e, :, chunk(t), :] = d
                fv0[c, e, :, chunk(t), :] = free * d
        return 0

    lax.fori_loop(0, NP - 1, stage_one, 0)

    def apply_sweep(ref, first_plane, last_plane, node):
        clear_carry()
        for t in range(CH):
            for c in range(3):
                for i, value in enumerate(full_transform(ref, c, first_plane, t)):
                    carry_t[t, 4 * c + i] = value

        def body(e, _):
            kept = None
            for t in range(CH):
                modes = []
                for c in range(3):
                    new = full_transform(ref, c, e + 1, t)
                    old = [carry_t[t, 4 * c + i] for i in range(4)]
                    for i, value in enumerate(new):
                        carry_t[t, 4 * c + i] = value
                    modes.append(element_modes(old, new))
                modulus = mod_e[e, :, chunk(t), :]
                forces = [{k: modulus * f for k, f in g.items()} for g in element_forces(modes)]
                applied, kept = scatter(t, forces, kept, None)
                free = fld[4, e, :, chunk(t), :]
                for c in range(3):
                    node(c, e, t, free, applied[c])
            return 0

        lax.fori_loop(first_plane, last_plane, body, 0)

    def node_two(c, e, t, free, applied):
        d = v0[c, e, :, chunk(t), :]
        r = rhs[c, e, :, chunk(t), :] - (free * applied + (1.0 - free) * d)
        new = (rho_one * rho_zero) * d + (2.0 * rho_one / delta) * r
        rhs[c, e, :, chunk(t), :] = r
        v1[c, e, :, chunk(t), :] = new
        fv1[c, e, :, chunk(t), :] = free * new

    apply_sweep(fv0, 1, NP - 2, node_two)

    for copy in sums1:
        copy.wait_recv()
    total = src1[...]
    for n in range(len(plane)):
        total = total + land1[n]
    src2[...] = total
    sums2 = []
    for n, d in enumerate(ring):
        copy = pltpu.make_async_remote_copy(
            src_ref=src2, dst_ref=land2.at[n], send_sem=s2.at[n], recv_sem=r2.at[n],
            device_id=at(d), device_id_type=MESH,
        )
        copy.start()
        sums2.append(copy)

    def node_three(c, e, t, free, applied):
        d = v1[c, e, :, chunk(t), :]
        r = rhs[c, e, :, chunk(t), :] - (free * applied + (1.0 - free) * d)
        new = (rho_two * rho_one) * d + (2.0 * rho_two / delta) * r
        adj[c, e, :, chunk(t), :] = v0[c, e, :, chunk(t), :] + d + new

    apply_sweep(fv1, 2, NP - 3, node_three)

    for t in range(CH):
        carry_p[t, 0] = zero
        for c in range(3):
            for i, value in enumerate(full_transform(adj, c, 3, t)):
                carry_t[t, 4 * c + i] = value
            for i, value in enumerate(full_transform(fld, c, 3, t)):
                carry_t[t, 12 + 4 * c + i] = value

    def stage_four(e, _):
        kept = None
        for t in range(CH):
            modes = []
            for ref, base in ((adj, 0), (fld, 12)):
                group = []
                for c in range(3):
                    new = full_transform(ref, c, e + 1, t)
                    old = [carry_t[t, base + 4 * c + i] for i in range(4)]
                    for i, value in enumerate(new):
                        carry_t[t, base + 4 * c + i] = value
                    group.append(element_modes(old, new))
                modes.append(group)
            forces = element_forces(modes[1])
            work = None
            for a, f in zip(modes[0], forces):
                for k, value in f.items():
                    work = a[k] * value if work is None else work + a[k] * value
            g = lead[e, :, chunk(t), :] - grow[e, :, chunk(t), :] * work
            share = g + carry_p[t, 0]
            carry_p[t, 0] = g
            share = share + z_prev(share)
            down, kept = y_gather(share, kept)
            sens[e, chunk(t), :] = (share + down)[0]
        return 0

    lax.fori_loop(3, W + BX, stage_four, 0)

    for copy in sums2:
        copy.wait_recv()
    total = src2[...]
    for n in range(len(ring)):
        total = total + land2[n]
    total = jnp.sum(jnp.sum(total, axis=0, keepdims=True), axis=1, keepdims=True)
    mean = total * (1.0 / float(BX * BY * BZ * sizes[0] * sizes[1] * sizes[2]))
    aggregate = jnp.sqrt(jnp.sqrt(jnp.sqrt(mean)))
    scale = jnp.broadcast_to(aggregate / (8.0 * mean), (8, 128))
    share = scale * 0.125
    for p in range(BX):
        for h in (0, 8):
            sens_out[p, h : h + 8, :] = share * sens[W + p, h + 4 : h + 12, :]
            for c in range(3):
                adj_out[c, p, h : h + 8, :] = scale * adj[c, W + p, 0, h + 4 : h + 12, :]

    for copy in halos + sums1 + sums2:
        copy.wait_send()


def local(sizes, displacement, density, solid, material, fixed):
    plane, ring = partners(sizes)
    f32, i32 = jnp.float32, jnp.int32
    vm = pltpu.VMEM
    dma = pltpu.SemaphoreType.DMA
    node = (3, NP, 2, ROWS, 128)
    scratch = [
        vm((3, BX, BY, BZ), f32), vm((BX, BY, BZ), f32), vm((BX, BY, BZ), i32), vm((BX, BY, BZ), i32), vm((BX, BY, BZ), i32),
        vm((6, BX, BY, BZ), f32), vm((6, 2, 8, 128), f32), vm((6, 2, 8, 128), f32),
        vm((16, 128), f32), vm((16, 128), f32), vm((8, 128), f32), vm((8, 128), f32),
        vm((2, 6, BX, BY, BZ), f32), vm((3, 2, 6, 2, 8, 128), f32), vm((3, 2, 16, 128), f32), vm((3, 2, 2, 8, 128), f32),
        vm((6, NP, 2, ROWS, 128), f32),
        vm((NP, 2, 24, 128), f32), vm((NP, 2, 24, 128), f32), vm((NP, 2, 24, 128), f32),
        vm(node, f32), vm(node, f32), vm(node, f32), vm(node, f32), vm(node, f32), vm(node, f32),
        vm((NP, 24, 128), f32),
        vm((CH, 24, 2, 8, 128), f32), vm((CH, 12, 2, 8, 128), f32),
        vm((8, 128), f32), vm((len(plane), 8, 128), f32), vm((8, 128), f32), vm((len(ring), 8, 128), f32),
        dma((5,)), dma((len(HALO),)), dma((len(HALO),)),
        dma((len(plane),)), dma((len(plane),)), dma((len(ring),)), dma((len(ring),)),
    ]
    return pl.pallas_call(
        functools.partial(kernel, sizes),
        out_shape=(jax.ShapeDtypeStruct((3, BX, BY, BZ), f32), jax.ShapeDtypeStruct((BX, BY, BZ), f32)),
        in_specs=[pl.BlockSpec(memory_space=pl.ANY)] * 5,
        out_specs=(pl.BlockSpec(memory_space=pltpu.VMEM), pl.BlockSpec(memory_space=pltpu.VMEM)),
        scratch_shapes=scratch,
        compiler_params=pltpu.CompilerParams(
            collective_id=0, has_side_effects=True, vmem_limit_bytes=40 * 1024 * 1024
        ),
    )(displacement, density, solid, material, fixed)


def solution(mesh):
    sizes = tuple(mesh.shape[a] for a in AXES)
    field = P(*AXES)
    vector = P(None, *AXES)
    return jax.shard_map(
        functools.partial(local, sizes),
        mesh=mesh,
        in_specs=(vector, field, field, field, field),
        out_specs=(vector, field),
        check_vma=False,
    )
```

profile of v0, /device:TPU:1, one launch (start us, length us, event | category | flops | bytes accessed | tf_op | source)
XLA Modules:
  0.0 45.7 jit_solution(13158127642450212561)
XLA Ops:
  0.6 0.0 copy-start
  0.6 0.9 %copy-done = f32[3,4,16,128]{3,2,1,0:T(8,128)S(1)} copy-done((f32[3,4,16,128]{3,2,1,0:T(8,128)S(1)}, f32[3,4,16,128]{3,2,1,0:T(8,128)}, u32[]{:S(2)}) %copy-start) | copy-done | bytes 98328
  1.5 0.0 copy-start.1
  1.5 0.8 %copy-done.1 = f32[4,16,128]{2,1,0:T(8,128)S(1)} copy-done((f32[4,16,128]{2,1,0:T(8,128)S(1)}, f32[4,16,128]{2,1,0:T(8,128)}, u32[]{:S(2)}) %copy-start.1) | copy-done | bytes 32792
  2.3 0.0 copy-start.2
  2.3 0.8 %copy-done.2 = s32[4,16,128]{2,1,0:T(8,128)S(1)} copy-done((s32[4,16,128]{2,1,0:T(8,128)S(1)}, s32[4,16,128]{2,1,0:T(8,128)}, u32[]{:S(2)}) %copy-start.2) | copy-done | bytes 32792
  3.0 0.0 copy-start.3
  3.0 0.8 %copy-done.3 = s32[4,16,128]{2,1,0:T(8,128)S(1)} copy-done((s32[4,16,128]{2,1,0:T(8,128)S(1)}, s32[4,16,128]{2,1,0:T(8,128)}, u32[]{:S(2)}) %copy-start.3) | copy-done | bytes 32792
  3.8 0.0 copy-start.4
  3.8 0.8 %copy-done.4 = s32[4,16,128]{2,1,0:T(8,128)S(1)} copy-done((s32[4,16,128]{2,1,0:T(8,128)S(1)}, s32[4,16,128]{2,1,0:T(8,128)}, u32[]{:S(2)}) %copy-start.4) | copy-done | bytes 32792
  4.6 39.8 %shard_map.68 = (f32[3,4,16,128]{3,2,1,0:T(8,128)S(1)}, f32[4,16,128]{2,1,0:T(8,128)S(1)}) custom-call(f32[3,4,16,128]{3,2,1,0:T(8,128)S(1)} %copy-done, f32[4,16,128]{2,1,0:T(8,128)S(1)} %copy-done.1, s32[4,16,128]{2,1,0:T(8,128)S(1)} %copy-done.2, s32[4,16,128]{2,1,0:T(8,128)S(1)} %copy-done.3, s32[4,16,128]{2,1,0:T(8,128)S(1)} %copy-done.4), custom_call_target="tpu_custom_call" | custom-call | tf_op jit(solution)/shard_map/pallas_call | solution.py:591
  44.4 0.6 %copy.9 = f32[3,4,16,128]{3,2,1,0:T(8,128)} copy(f32[3,4,16,128]{3,2,1,0:T(8,128)S(1)} %get-tuple-element.4) | data formatting | bytes 196608
  45.0 0.6 %copy.10 = f32[4,16,128]{2,1,0:T(8,128)} copy(f32[4,16,128]{2,1,0:T(8,128)S(1)} %get-tuple-element.5) | data formatting | bytes 65536
Async XLA Ops:
  0.6 0.9 %copy-start = (f32[3,4,16,128]{3,2,1,0:T(8,128)S(1)}, f32[3,4,16,128]{3,2,1,0:T(8,128)}, u32[]{:S(2)}) copy-start(f32[3,4,16,128]{3,2,1,0:T(8,128)} %disp_in.1) | copy-start | bytes 294916
  1.5 0.8 %copy-start.1 = (f32[4,16,128]{2,1,0:T(8,128)S(1)}, f32[4,16,128]{2,1,0:T(8,128)}, u32[]{:S(2)}) copy-start(f32[4,16,128]{2,1,0:T(8,128)} %dens_in.1) | copy-start | bytes 98308
  2.3 0.8 %copy-start.2 = (s32[4,16,128]{2,1,0:T(8,128)S(1)}, s32[4,16,128]{2,1,0:T(8,128)}, u32[]{:S(2)}) copy-start(s32[4,16,128]{2,1,0:T(8,128)} %solid_in.1) | copy-start | bytes 98308
  3.0 0.8 %copy-start.3 = (s32[4,16,128]{2,1,0:T(8,128)S(1)}, s32[4,16,128]{2,1,0:T(8,128)}, u32[]{:S(2)}) copy-start(s32[4,16,128]{2,1,0:T(8,128)} %mat_in.1) | copy-start | bytes 98308
  3.8 0.8 %copy-start.4 = (s32[4,16,128]{2,1,0:T(8,128)S(1)}, s32[4,16,128]{2,1,0:T(8,128)}, u32[]{:S(2)}) copy-start(s32[4,16,128]{2,1,0:T(8,128)} %fixed_in.1) | copy-start | bytes 98308
where the time goes:
time: 46.1 us; the launch traced here: 45.7 us
  Pallas kernels  39.8 us (86%)
  local copies, waits for them, and re-layouts  5.17 us (11%)
  between operations  0.65 us (1%)
    pallas_call x1, Pallas kernels, local(): pl.pallas_call(functools.partial(kernel, sizes), out_shape=(jax.ShapeDtyp...  39.8 us
    unnamed x12, local copies, waits for them, and re-layouts  5.17 us

commit v1 on v0

v1 whole, which is shorter than its diff:
```python
import functools
import itertools

import jax
import jax.numpy as jnp
import numpy as np
from jax import lax
from jax.experimental import pallas as pl
from jax.experimental.pallas import tpu as pltpu
from jax.sharding import PartitionSpec as P

POISSON = 0.3
VOID_FLOOR = 0.001
MODULI = (1.0, 0.7, 0.45, 0.25)
MESH = pl.DeviceIdType.MESH
AXES = ("gx", "gy", "gz")

BX, BY, BZ = 4, 16, 128
W = 4
NP = BX + 2 * W
ROWS = 40
UNITS = 4
GROUP = 24


def lame_pair():
    first = POISSON / ((1.0 + POISSON) * (1.0 - 2.0 * POISSON))
    shear = 1.0 / (2.0 * (1.0 + POISSON))
    return (first, shear)


def corner_signs():
    return [(2 * a - 1, 2 * b - 1, 2 * c - 1) for a in (0, 1) for b in (0, 1) for c in (0, 1)]


def element_table():
    first, shear = lame_pair()
    elastic = np.zeros((6, 6))
    elastic[:3, :3] = first
    for index in range(3):
        elastic[index, index] += 2.0 * shear
        elastic[index + 3, index + 3] = shear
    point = 1.0 / np.sqrt(3.0)
    matrix = np.zeros((24, 24))
    for xi in (-point, point):
        for eta in (-point, point):
            for zeta in (-point, point):
                strain = np.zeros((6, 24))
                for index, signs in enumerate(corner_signs()):
                    sa, sb, sc = signs
                    gradx = 2.0 * sa * (1 + sb * eta) * (1 + sc * zeta) / 8.0
                    grady = 2.0 * sb * (1 + sa * xi) * (1 + sc * zeta) / 8.0
                    gradz = 2.0 * sc * (1 + sa * xi) * (1 + sb * eta) / 8.0
                    strain[0, index] = gradx
                    strain[1, 8 + index] = grady
                    strain[2, 16 + index] = gradz
                    strain[3, 8 + index] = gradz
                    strain[3, 16 + index] = grady
                    strain[4, index] = gradz
                    strain[4, 16 + index] = gradx
                    strain[5, index] = grady
                    strain[5, 8 + index] = gradx
                matrix += strain.T @ elastic @ strain / 8.0
    return matrix


def chebyshev_constants():
    rowsum = float(np.max(np.sum(np.abs(element_table()), axis=1)))
    upper = max(2.0, 8.0 * max(MODULI) * rowsum)
    lower = upper / 20.0
    theta = (upper + lower) / 2.0
    delta = (upper - lower) / 2.0
    sigma = theta / delta
    rho_zero = 1.0 / sigma
    rho_one = 1.0 / (2.0 * sigma - rho_zero)
    rho_two = 1.0 / (2.0 * sigma - rho_one)
    return (theta, delta, rho_zero, rho_one, rho_two)


HALO = [d for d in itertools.product((-1, 0, 1), repeat=3) if d != (0, 0, 0)]
FIRST = [(-1, -1, -1), (0, -1, -1), (-1, 0, -1), (-1, -1, 0), (-1, 0, 0), (0, 0, -1), (0, -1, 0)]
LATER = sorted((d for d in HALO if d not in FIRST), key=lambda d: (-abs(d[0]) - abs(d[1]) - abs(d[2])))


def partners(sizes):
    nx, ny, nz = sizes

    def far(d):
        return sum(min(o % n, -o % n) for o, n in zip(d, sizes))

    plane = [(a, 0, c) for a in range(nx) for c in range(nz) if (a, c) != (0, 0)]
    ring = [(0, b, 0) for b in range(1, ny)]
    return sorted(plane, key=far, reverse=True), sorted(ring, key=far, reverse=True)


GREETED = [(0, 7, 0), (0, -7, 0), (0, 4, 0), (0, -4, 0), (3, 0, 2), (-3, 0, 2), (3, 0, 0), (-3, 0, 0)]


def rows_of():
    return lax.broadcasted_iota(jnp.int32, (8, 128), 0)


def z_next(x):
    return pltpu.roll(x, 127, 1)


def z_prev(x):
    return pltpu.roll(x, 1, 1)


def unit_rows(t):
    return slice(32, 40) if t == 3 else slice(8 * t, 8 * t + 8)


def element_rows(t):
    return slice(8 * t, 8 * t + 8)


def y_transform(ref, comp, plane, t):
    a = ref[comp, plane, unit_rows(t), :]
    if t < 3:
        b = ref[comp, plane, 8 * t + 1 : 8 * t + 9, :]
    else:
        r = pltpu.roll(a, 7, 0)
        b = jnp.where(rows_of() == 7, pltpu.roll(r, 128 - GROUP, 1), r)
    return a + b, b - a


def full_transform(ref, comp, plane, t):
    s, d = y_transform(ref, comp, plane, t)
    sn, dn = z_next(s), z_next(d)
    return [s + sn, sn - s, d + dn, dn - d]


def central_transform(ref, comp, plane, t):
    s, d = y_transform(ref, comp, plane, t)
    sn, dn = z_next(s), z_next(d)
    return [s + sn, sn - s, d + dn]


def central_gradients(old, new):
    return [new[0] - old[0], old[2] + new[2], old[1] + new[1]]


def stress_of(grads):
    first, shear = lame_pair()
    exx, eyy, ezz = grads[0][0], grads[1][1], grads[2][2]
    base = first * (exx + eyy + ezz)
    sxx, syy, szz = base + 2.0 * shear * exx, base + 2.0 * shear * eyy, base + 2.0 * shear * ezz
    syz = shear * (grads[1][2] + grads[2][1])
    sxz = shear * (grads[0][2] + grads[2][0])
    sxy = shear * (grads[0][1] + grads[1][0])
    return sxx, syy, szz, syz, sxz, sxy


def unit_of(s):
    sxx, syy, szz, syz, sxz, sxy = s
    return (
        sxx * sxx + syy * syy + szz * szz - sxx * syy - syy * szz - szz * sxx
        + 3.0 * (syz * syz + sxz * sxz + sxy * sxy)
    )


def element_modes(old, new):
    ss, sd, ds, dd = zip(old, new)
    return {
        "DSS": ss[1] - ss[0], "SSD": sd[0] + sd[1], "DSD": sd[1] - sd[0], "SDS": ds[0] + ds[1],
        "DDS": ds[1] - ds[0], "SDD": dd[0] + dd[1], "DDD": dd[1] - dd[0],
    }


def element_forces(modes):
    first, shear = lame_pair()
    u, v, w = modes
    s = stress_of([[m["DSS"], m["SDS"], m["SSD"]] for m in (u, v, w)])
    sxx, syy, szz, syz, sxz, sxy = [x * (1.0 / 16.0) for x in s]
    own, cross = (first + 3.0 * shear) / 48.0, first / 48.0
    twist, cube = shear / 48.0, (first + 4.0 * shear) / 144.0

    def pair(a, b):
        return own * a + cross * b, cross * a + own * b

    u_xy, w_yz = pair(u["DDS"], w["SDD"])
    u_xz, v_yz = pair(u["DSD"], v["SDD"])
    v_xy, w_xz = pair(v["DDS"], w["DSD"])
    every = u["SDD"] + v["DSD"] + w["DDS"]
    return [
        {"DSS": sxx, "SDS": sxy, "SSD": sxz, "DDS": u_xy, "DSD": u_xz,
         "SDD": twist * (every + u["SDD"]), "DDD": cube * u["DDD"]},
        {"DSS": sxy, "SDS": syy, "SSD": syz, "DDS": v_xy, "SDD": v_yz,
         "DSD": twist * (every + v["DSD"]), "DDD": cube * v["DDD"]},
        {"DSS": sxz, "SDS": syz, "SSD": szz, "SDD": w_yz, "DSD": w_xz,
         "DDS": twist * (every + w["DDS"]), "DDD": cube * w["DDD"]},
    ]


def y_prev(value, kept, t):
    r = pltpu.roll(value, 1, 0)
    if t == 0:
        return r, r
    before = kept if t < 3 else pltpu.roll(r, GROUP, 1)
    return jnp.where(rows_of() == 0, before, r), r


def kernel(sizes, disp_in, dens_in, solid_in, mat_in, fixed_in, adj_out, sens_out,
           disp_v, dens_v, solid_v, mat_v, fixed_v, own, ylow, yhigh, zlow, zhigh, zlow_y, zhigh_y, yfirst,
           rx, ry, rz, ryz, rxf, ryf, strip, tm, tn, fld, mod_e, grow, lead, rhs, v0, fv0, v1, fv1, adj, sens, merged,
           carry_t, carry_p, src1, land1, src2, land2, in_sem, send_sem, recv_sem, s1, r1, s2, r2):
    position = [lax.axis_index(a) for a in AXES]

    def at(d):
        return tuple(lax.rem(p + (o % n), n) if o % n else p for p, o, n in zip(position, d, sizes))

    plane, ring = partners(sizes)
    theta, delta, rho_zero, rho_one, rho_two = chebyshev_constants()

    loads = [
        pltpu.make_async_copy(src, dst, in_sem.at[n])
        for n, (src, dst) in enumerate(
            ((disp_in, disp_v), (fixed_in, fixed_v), (dens_in, dens_v), (mat_in, mat_v), (solid_in, solid_v))
        )
    ]
    for copy in loads:
        copy.start()
    barrier = pltpu.get_barrier_semaphore()
    greeted = GREETED + LATER + FIRST
    for d in greeted:
        pl.semaphore_signal(barrier, inc=1, device_id=at(d), device_id_type=MESH)
    for copy in loads:
        copy.wait()

    free = 1.0 - fixed_v[...].astype(jnp.float32)
    own[4] = free
    own[3] = dens_v[...]
    for c in range(3):
        own[c] = disp_v[c] * free
    material = mat_v[...]
    scale_class = jnp.zeros(material.shape, jnp.float32)
    for index in range(4):
        scale_class = scale_class + jnp.where(material == index, MODULI[index], 0.0).astype(jnp.float32)
    own[5] = scale_class * (VOID_FLOOR + (1.0 - VOID_FLOOR) * solid_v[...].astype(jnp.float32))

    lane16 = lax.broadcasted_iota(jnp.int32, (16, 128), 1)
    lane8 = lax.broadcasted_iota(jnp.int32, (8, 128), 1)

    def pack_lanes(first_lane, ref, ref_y):
        packed = jnp.zeros((16, 128), jnp.float32)
        for f in range(6):
            for p in range(BX):
                group = 4 * (BX * f + p)
                shift = (group - first_lane) % 128
                block = own[f, p]
                packed = jnp.where(lane16 < group, packed, pltpu.roll(block, shift, 1) if shift else block)
        ref[...] = packed
        ref_y[0:4, :] = packed[0:4]
        ref_y[4:8, :] = packed[12:16]

    pack_lanes(0, zlow, zlow_y)
    for f in range(4):
        for p in range(BX):
            yfirst[BX * f + p : BX * f + p + 1, :] = own[f, p, 0:1, :]

    pl.semaphore_wait(barrier, len(greeted))

    def send(src, dst, d, sems, n, group):
        copy = pltpu.make_async_remote_copy(
            src_ref=src, dst_ref=dst, send_sem=sems[0].at[n], recv_sem=sems[1].at[n],
            device_id=at(d), device_id_type=MESH,
        )
        copy.start()
        group.append(copy)

    halo_sems = (send_sem, recv_sem)
    first, later = [], []
    for n, (dx, dy, dz) in enumerate(FIRST):
        sx = 1 - dx
        if dz:
            src, dst = (zlow_y, ryz.at[sx, 1, 1]) if dy else (zlow, rz.at[sx, 1])
        else:
            src, dst = (yfirst, ryf.at[sx - 1]) if dy else (own.at[pl.ds(0, 4), 0], rxf)
        send(src, dst, (dx, dy, dz), halo_sems, n, first)

    pack_lanes(124, zhigh, zhigh_y)
    for f in range(6):
        for p in range(BX):
            half = 4 * (p % 2)
            ylow[f, p // 2, half : half + 4, :] = own[f, p, 0:4, :]
            yhigh[f, p // 2, half : half + 4, :] = own[f, p, 12:16, :]
    rest = [d for d in HALO if d not in FIRST or d[2] == 0]
    rest.sort(key=lambda d: (d[2] != 0, d[1] != 0))
    for n, (dx, dy, dz) in enumerate(rest):
        sx, sy, sz = 1 - dx, (1 - dy) // 2, (1 - dz) // 2
        if dz == 0 and dy == 0:
            src, dst = own, rx.at[sx // 2]
        elif dz == 0:
            src, dst = (yhigh if dy > 0 else ylow), ry.at[sx, sy]
        elif dy == 0:
            src, dst = (zhigh if dz > 0 else zlow), rz.at[sx, sz]
        else:
            src, dst = (zhigh_y if dz > 0 else zlow_y), ryz.at[sx, sy, sz]
        send(src, dst, (dx, dy, dz), halo_sems, len(FIRST) + n, later)

    zero = jnp.zeros((8, 128), jnp.float32)

    def clear(p, _):
        for f in range(6):
            fld[f, p, 24:32, :] = zero
        for c in range(3):
            fv0[c, p, 24:32, :] = zero
            fv1[c, p, 24:32, :] = zero
            adj[c, p, 24:32, :] = zero
        return 0

    lax.fori_loop(0, NP, clear, 0)

    def inside(axis, o):
        if o == 0:
            return 1.0
        edge = 0 if o < 0 else sizes[axis] - 1
        return jnp.where(position[axis] == edge, 0.0, 1.0).astype(jnp.float32)

    for copy in first:
        copy.wait_recv()
    in_x, in_y, in_z = inside(0, 1), inside(1, 1), inside(2, 1)
    strips = [(rz[1, 1] * in_z, ryz[1, 1, 1] * (in_y * in_z)),
              (rz[2, 1] * (in_x * in_z), ryz[2, 1, 1] * (in_x * in_y * in_z))]
    for f in range(4):
        for p in range(BX + 1):
            far = p // BX
            group = 4 * (BX * f + p % BX)
            block = rxf[f] * in_x if far else own[f, p]
            line = ryf[far, BX * f + p % BX : BX * f + p % BX + 1, :] * (in_y * in_x if far else in_y)
            line = jnp.broadcast_to(line, (8, 128))
            tm[f, p, 0:16, :] = block
            tm[f, p, 16:24, :] = line
            z16, z8 = strips[far]
            tn[f, p, 0:16, :] = jnp.where(lane16 == 127, pltpu.roll(z16, 127 - group, 1), z_next(block))
            tn[f, p, 16:24, :] = jnp.where(lane8 == 127, pltpu.roll(z8, 127 - group, 1), z_next(line))

    partial = zero
    for start in (0, 8):
        old = None
        for p in range(BX + 1):
            new = []
            for f in range(4):
                a, an = tm[f, p, start : start + 8, :], tn[f, p, start : start + 8, :]
                b, bn = tm[f, p, start + 1 : start + 9, :], tn[f, p, start + 1 : start + 9, :]
                s, sn = a + b, an + bn
                new.append([s + sn, sn - s, (b - a) + (bn - an)])
            if old is not None:
                grads = [[0.25 * g for g in central_gradients(old[c], new[c])] for c in range(3)]
                rho = (old[3][0] + new[3][0]) * 0.125
                modulus = rho * rho * rho * own[5, p - 1, start : start + 8, :]
                q = modulus * modulus * unit_of(stress_of(grads))
                q = q * q
                partial = partial + q * q
            old = new
    src1[...] = partial
    sums1, sums2 = [], []
    for n, d in enumerate(plane):
        send(src1, land1.at[n], d, (s1, r1), n, sums1)

    for copy in later:
        copy.wait_recv()
    for sx in range(3):
        for sz in range(2):
            f_xz = inside(0, sx - 1) * inside(2, 2 * sz - 1)
            strip[sx, sz, 0:4, :] = ryz[sx, 0, sz, 4:8, :] * (f_xz * inside(1, -1))
            strip[sx, sz, 4:20, :] = rz[sx, sz] * f_xz
            strip[sx, sz, 20:24, :] = ryz[sx, 1, sz, 0:4, :] * (f_xz * inside(1, 1))

    def flush(stores):
        for ref, index, value in stores:
            ref[index] = value

    upper_half = rows_of() < 4

    def unpack(f, _):
        for sx in range(3):
            fx = inside(0, sx - 1)
            stores = []
            for p in range(BX):
                q = BX * sx + p
                a, b = [own[f, p, h : h + 8, :] if sx == 1 else rx[sx // 2, f, p, h : h + 8, :] * fx for h in (0, 8)]
                a, b = pltpu.roll(a, 4, 0), pltpu.roll(b, 4, 0)
                over, under = ry[sx, 0, f, p // 2] * (fx * inside(1, -1)), ry[sx, 1, f, p // 2] * (fx * inside(1, 1))
                if p % 2:
                    over = pltpu.roll(over, 4, 0)
                else:
                    under = pltpu.roll(under, 4, 0)
                chunks = [jnp.where(upper_half, over, a), jnp.where(upper_half, a, b), jnp.where(upper_half, b, under)]
                group = 4 * (BX * f + p)
                ends = None
                for t in range(3):
                    base = GROUP * t
                    below, above = strip[sx, 0, 8 * t : 8 * t + 8, :], strip[sx, 1, 8 * t : 8 * t + 8, :]
                    value = jnp.where(lane8 < base + 12, pltpu.roll(above, lax.rem(base + 8 + 128 - group, 128), 1),
                                      pltpu.roll(below, lax.rem(base + 12 + 128 - group, 128), 1))
                    value = jnp.where(lane8 < base + 8, pltpu.roll(chunks[t], base + 8, 1), value)
                    value = jnp.where(lane8 < base + 16, value, pltpu.roll(chunks[t], base + 16, 1))
                    ends = value if ends is None else jnp.where(lane8 < base, ends, value)
                    stores.append((fld, (f, q, slice(8 * t, 8 * t + 8)), chunks[t]))
                stores.append((fld, (f, q, slice(32, 40)), ends))
            flush(stores)
        return 0

    lax.fori_loop(0, 6, unpack, 0)

    kinds = ("SS", "SD", "DS", "DD")

    def scatter(t, forces, kept, stores):
        result, keep = [], []
        for c in range(3):
            by = {}
            for i, k in enumerate(kinds):
                s, d = forces[c].get("S" + k), forces[c].get("D" + k)
                if s is None and d is None:
                    continue
                if s is None:
                    by[k] = carry_p[t, 4 * c + i] - d
                    upper = d
                elif d is None:
                    by[k] = carry_p[t, 4 * c + i] + s
                    upper = s
                else:
                    by[k] = carry_p[t, 4 * c + i] + (s - d)
                    upper = s + d
                stores.append((carry_p, (t, 4 * c + i), upper))
            rows = []
            for k in ("S", "D"):
                s, d = by[k + "S"], by.get(k + "D")
                rows.append(s + z_prev(s) if d is None else (s - d) + z_prev(s + d))
            down, r = y_prev(rows[0] + rows[1], None if kept is None else kept[c], t)
            result.append((rows[0] - rows[1]) + down)
            keep.append(r)
        return result, keep

    def clear_carry():
        for i in range(12):
            for t in range(UNITS):
                carry_p[t, i] = zero

    clear_carry()
    for t in range(UNITS):
        for c in range(3):
            for i, value in enumerate(central_transform(fld, c, 0, t)):
                carry_t[t, 4 * c + i] = value
        s, _d = y_transform(fld, 3, 0, t)
        carry_t[t, 12] = s + z_next(s)

    def stage_one(e, _):
        kept, stores = None, []
        first, shear = lame_pair()
        for t in range(UNITS):
            nodes, cells = unit_rows(t), element_rows(t)
            grads = []
            for c in range(3):
                new = central_transform(fld, c, e + 1, t)
                old = [carry_t[t, 4 * c + i] for i in range(3)]
                stores += [(carry_t, (t, 4 * c + i), value) for i, value in enumerate(new)]
                grads.append([0.25 * g for g in central_gradients(old, new)])
            s, _d = y_transform(fld, 3, e + 1, t)
            mass = s + z_next(s)
            rho = (carry_t[t, 12] + mass) * 0.125
            rho_stiff = rho * rho * fld[5, e, nodes, :]
            modulus = rho_stiff * rho
            growth = 3.0 * rho_stiff
            stress = stress_of(grads)
            unit = unit_of(stress)
            square = modulus * modulus
            q = square * unit
            q3 = q * q * q
            stores += [
                (carry_t, (t, 12), mass), (mod_e, (e, cells), modulus), (grow, (e, cells), growth),
                (lead, (e, cells), growth * (8.0 * q3 * modulus * unit)),
            ]
            sxx, syy, szz, syz, sxz, sxy = stress
            weight = q3 * square
            trace = sxx + syy + szz
            hxx, hyy, hzz = 3.0 * sxx - trace, 3.0 * syy - trace, 3.0 * szz - trace
            base = first * (hxx + hyy + hzz)
            wxx = weight * (base + 2.0 * shear * hxx)
            wyy = weight * (base + 2.0 * shear * hyy)
            wzz = weight * (base + 2.0 * shear * hzz)
            skew = weight * (6.0 * shear)
            wyz, wxz, wxy = skew * syz, skew * sxz, skew * sxy
            load, kept = scatter(t, [
                {"DSS": wxx, "SDS": wxy, "SSD": wxz},
                {"DSS": wxy, "SDS": wyy, "SSD": wyz},
                {"DSS": wxz, "SDS": wyz, "SSD": wzz},
            ], kept, stores)
            free = fld[4, e, nodes, :]
            for c in range(3):
                r = free * load[c]
                d = r * (1.0 / theta)
                stores += [(rhs, (c, e, nodes), r), (v0, (c, e, nodes), d), (fv0, (c, e, nodes), free * d)]
        flush(stores)
        return 0

    lax.fori_loop(0, NP - 1, stage_one, 0)

    def apply_sweep(ref, first_plane, last_plane, node):
        clear_carry()
        for t in range(UNITS):
            for c in range(3):
                for i, value in enumerate(full_transform(ref, c, first_plane, t)):
                    carry_t[t, 4 * c + i] = value

        def body(e, _):
            kept, stores = None, []
            for t in range(UNITS):
                modes = []
                for c in range(3):
                    new = full_transform(ref, c, e + 1, t)
                    old = [carry_t[t, 4 * c + i] for i in range(4)]
                    stores += [(carry_t, (t, 4 * c + i), value) for i, value in enumerate(new)]
                    modes.append(element_modes(old, new))
                modulus = mod_e[e, element_rows(t), :]
                forces = [{k: modulus * f for k, f in g.items()} for g in element_forces(modes)]
                applied, kept = scatter(t, forces, kept, stores)
                free = fld[4, e, unit_rows(t), :]
                for c in range(3):
                    node(c, e, unit_rows(t), free, applied[c], stores)
            flush(stores)
            return 0

        lax.fori_loop(first_plane, last_plane, body, 0)

    def node_two(c, e, rows, free, applied, stores):
        d = v0[c, e, rows, :]
        r = rhs[c, e, rows, :] - (free * applied + (1.0 - free) * d)
        new = (rho_one * rho_zero) * d + (2.0 * rho_one / delta) * r
        stores += [(rhs, (c, e, rows), r), (v1, (c, e, rows), new), (fv1, (c, e, rows), free * new)]

    apply_sweep(fv0, 1, NP - 2, node_two)

    for copy in sums1:
        copy.wait_recv()
    total = src1[...]
    for n in range(len(plane)):
        total = total + land1[n]
    src2[...] = total
    for n, d in enumerate(ring):
        send(src2, land2.at[n], d, (s2, r2), n, sums2)

    def node_three(c, e, rows, free, applied, stores):
        d = v1[c, e, rows, :]
        r = rhs[c, e, rows, :] - (free * applied + (1.0 - free) * d)
        new = (rho_two * rho_one) * d + (2.0 * rho_two / delta) * r
        stores.append((adj, (c, e, rows), v0[c, e, rows, :] + d + new))

    apply_sweep(fv1, 2, NP - 3, node_three)

    for t in range(UNITS):
        carry_p[t, 0] = zero
        for c in range(3):
            for i, value in enumerate(full_transform(adj, c, W - 1, t)):
                carry_t[t, 4 * c + i] = value
            for i, value in enumerate(full_transform(fld, c, W - 1, t)):
                carry_t[t, 12 + 4 * c + i] = value

    def stage_four(e, _):
        kept, stores = None, []
        for t in range(UNITS):
            modes = []
            for ref, base in ((fld, 12), (adj, 0)):
                group = []
                for c in range(3):
                    new = full_transform(ref, c, e + 1, t)
                    old = [carry_t[t, base + 4 * c + i] for i in range(4)]
                    stores += [(carry_t, (t, base + 4 * c + i), value) for i, value in enumerate(new)]
                    group.append(element_modes(old, new))
                modes.append(group if ref is adj else element_forces(group))
            work = None
            for f, a in zip(*modes):
                for k, value in f.items():
                    work = a[k] * value if work is None else work + a[k] * value
            g = lead[e, element_rows(t), :] - grow[e, element_rows(t), :] * work
            share = g + carry_p[t, 0]
            share = share + z_prev(share)
            down, kept = y_prev(share, kept, t)
            stores += [(carry_p, (t, 0), g), (sens, (e, element_rows(t)), share + down)]
        flush(stores)
        return 0

    lax.fori_loop(W - 1, W + BX, stage_four, 0)

    for c in range(4):
        for p in range(BX):
            main, ends = ((sens.at[W + p], sens[W + p, 24:32, :]) if c == 3 else (adj.at[c, W + p], adj[c, W + p, 32:40, :]))
            for t in range(3):
                base = GROUP * t
                value = jnp.where(lane8 < 4, pltpu.roll(ends, (128 - 16 - base) % 128, 1), main[8 * t : 8 * t + 8, :])
                merged[c, p, 8 * t : 8 * t + 8, :] = jnp.where(
                    lane8 >= 124, pltpu.roll(ends, (120 - base) % 128, 1), value
                )

    for copy in sums2:
        copy.wait_recv()
    total = src2[...]
    for n in range(len(ring)):
        total = total + land2[n]
    total = jnp.sum(jnp.sum(total, axis=0, keepdims=True), axis=1, keepdims=True)
    mean = total * (1.0 / float(BX * BY * BZ * sizes[0] * sizes[1] * sizes[2]))
    aggregate = jnp.sqrt(jnp.sqrt(jnp.sqrt(mean)))
    scale = jnp.broadcast_to(aggregate / (8.0 * mean), (8, 128))
    share = scale * 0.125
    for p in range(BX):
        for h in (0, 8):
            sens_out[p, h : h + 8, :] = share * merged[3, p, h + 4 : h + 12, :]
            for c in range(3):
                adj_out[c, p, h : h + 8, :] = scale * merged[c, p, h + 4 : h + 12, :]

    for copy in first + later + sums1 + sums2:
        copy.wait_send()


def hand_over(adj_in, sens_in, adj_out, sens_out, sems):
    copies = [pltpu.make_async_copy(adj_in, adj_out, sems.at[0]), pltpu.make_async_copy(sens_in, sens_out, sems.at[1])]
    for copy in copies:
        copy.start()
    for copy in copies:
        copy.wait()


def local(sizes, displacement, density, solid, material, fixed):
    plane, ring = partners(sizes)
    f32, i32 = jnp.float32, jnp.int32
    vm = pltpu.VMEM
    dma = pltpu.SemaphoreType.DMA
    node = (3, NP, ROWS, 128)
    element = (NP, 32, 128)
    tile = (8, 128)
    messages = len(HALO) + 3
    scratch = [
        vm((3, BX, BY, BZ), f32), vm((BX, BY, BZ), f32), vm((BX, BY, BZ), i32), vm((BX, BY, BZ), i32), vm((BX, BY, BZ), i32),
        vm((6, BX, BY, BZ), f32), vm((6, 2, 8, 128), f32), vm((6, 2, 8, 128), f32),
        vm((16, 128), f32), vm((16, 128), f32), vm(tile, f32), vm(tile, f32), vm((16, 128), f32),
        vm((2, 6, BX, BY, BZ), f32), vm((3, 2, 6, 2, 8, 128), f32), vm((3, 2, 16, 128), f32), vm((3, 2, 2, 8, 128), f32),
        vm((4, 16, 128), f32), vm((2, 16, 128), f32),
        vm((3, 2, 24, 128), f32), vm((4, BX + 1, 24, 128), f32), vm((4, BX + 1, 24, 128), f32),
        vm((6, NP, ROWS, 128), f32),
        vm(element, f32), vm(element, f32), vm(element, f32),
        vm(node, f32), vm(node, f32), vm(node, f32), vm(node, f32), vm(node, f32), vm(node, f32),
        vm(element, f32), vm((4, BX, 24, 128), f32),
        vm((UNITS, 24, 8, 128), f32), vm((UNITS, 12, 8, 128), f32),
        vm(tile, f32), vm((len(plane), 8, 128), f32), vm(tile, f32), vm((len(ring), 8, 128), f32),
        dma((5,)), dma((messages,)), dma((messages,)),
        dma((len(plane),)), dma((len(plane),)), dma((len(ring),)), dma((len(ring),)),
    ]
    outs = (jax.ShapeDtypeStruct((3, BX, BY, BZ), f32), jax.ShapeDtypeStruct((BX, BY, BZ), f32))
    results = pl.pallas_call(
        functools.partial(kernel, sizes),
        out_shape=outs,
        in_specs=[pl.BlockSpec(memory_space=pltpu.HBM)] * 5,
        out_specs=(pl.BlockSpec(memory_space=pltpu.VMEM), pl.BlockSpec(memory_space=pltpu.VMEM)),
        scratch_shapes=scratch,
        compiler_params=pltpu.CompilerParams(
            collective_id=0, has_side_effects=True, vmem_limit_bytes=40 * 1024 * 1024
        ),
    )(*[pltpu.with_memory_space_constraint(x, pltpu.HBM) for x in (displacement, density, solid, material, fixed)])
    return pl.pallas_call(
        hand_over,
        out_shape=outs,
        in_specs=[pl.BlockSpec(memory_space=pl.ANY)] * 2,
        out_specs=(pl.BlockSpec(memory_space=pltpu.HBM), pl.BlockSpec(memory_space=pltpu.HBM)),
        scratch_shapes=[dma((2,))],
    )(*[pltpu.with_memory_space_constraint(x, pltpu.VMEM) for x in results])


def solution(mesh):
    sizes = tuple(mesh.shape[a] for a in AXES)
    field = P(*AXES)
    vector = P(None, *AXES)
    return jax.shard_map(
        functools.partial(local, sizes),
        mesh=mesh,
        in_specs=(vector, field, field, field, field),
        out_specs=(vector, field),
        check_vma=False,
    )
```

time: 46.1 us -> 42.3 us (0.918)
  local copies, waits for them, and re-layouts: 5.17 us -> 0 us
  Pallas kernels: 39.8 us -> 41.5 us
    unnamed x12 -> x0, local copies, waits for them, and re-layouts: 5.17 us -> none
    pallas_call x1 -> x2, Pallas kernels: 39.8 us -> 41.5 us  [the longest x1 40.9 us: local(): pl.pallas_call(functools.partial(kernel, sizes), out_shape=outs, in_specs...]
where the time goes in v1:
time: 42.3 us; the launch traced here: 42.2 us
  Pallas kernels  41.5 us (98%)
  between operations  0.64 us (2%)
    pallas_call x1, Pallas kernels, local(): pl.pallas_call(functools.partial(kernel, sizes), out_shape=outs, in_specs...  40.9 us

profile of v1, /device:TPU:1, one launch (start us, length us, event | category | flops | bytes accessed | tf_op | source)
XLA Modules:
  0.0 42.2 jit_solution(15943538221954772440)
XLA Ops:
  0.6 40.9 %shard_map.68 = (f32[3,4,16,128]{3,2,1,0:T(8,128)S(1)}, f32[4,16,128]{2,1,0:T(8,128)S(1)}) custom-call(f32[3,4,16,128]{3,2,1,0:T(8,128)} %disp_in.1, f32[4,16,128]{2,1,0:T(8,128)} %dens_in.1, s32[4,16,128]{2,1,0:T(8,128)} %solid_in.1, s32[4,16,128]{2,1,0:T(8,128)} %mat_in.1, s32[4,16,128]{2,1,0:T(8,128)} %fixed_in.1), custom_call_target="tpu_custom_call" | custom-call | tf_op jit(solution)/shard_map/pallas_call | solution.py:652
  41.5 0.7 %shard_map.69 = (f32[3,4,16,128]{3,2,1,0:T(8,128)}, f32[4,16,128]{2,1,0:T(8,128)}) custom-call(f32[3,4,16,128]{3,2,1,0:T(8,128)S(1)} %get-tuple-element.4.adj_in, f32[4,16,128]{2,1,0:T(8,128)S(1)} %get-tuple-element.5.sens_in), custom_call_target="tpu_custom_call" | custom-call | tf_op jit(solution)/shard_map/pallas_call | solution.py:662

commit v2 on v1

--- a/solution.py
+++ b/solution.py
@@ -18,7 +18,7 @@
 BX, BY, BZ = 4, 16, 128
 W = 4
 NP = BX + 2 * W
-ROWS = 40
+ROWS = 48
 UNITS = 4
 GROUP = 24
 
@@ -79,7 +79,9 @@
 
 HALO = [d for d in itertools.product((-1, 0, 1), repeat=3) if d != (0, 0, 0)]
 FIRST = [(-1, -1, -1), (0, -1, -1), (-1, 0, -1), (-1, -1, 0), (-1, 0, 0), (0, 0, -1), (0, -1, 0)]
-LATER = sorted((d for d in HALO if d not in FIRST), key=lambda d: (-abs(d[0]) - abs(d[1]) - abs(d[2])))
+REST = [d for d in HALO if d not in FIRST or d[2] == 0]
+REST.sort(key=lambda d: (d[1] != 0 or d[2] != 0, d[0] != 0, d[2] != 0))
+LATER = [d for d in HALO if d not in FIRST]
 
 
 def partners(sizes):
@@ -93,11 +95,11 @@
     return sorted(plane, key=far, reverse=True), sorted(ring, key=far, reverse=True)
 
 
-GREETED = [(0, 7, 0), (0, -7, 0), (0, 4, 0), (0, -4, 0), (3, 0, 2), (-3, 0, 2), (3, 0, 0), (-3, 0, 0)]
-
-
-def rows_of():
-    return lax.broadcasted_iota(jnp.int32, (8, 128), 0)
+ROUNDS = [
+    [d for d in HALO if d[1] == 0] + [(0, 1, 0), (0, -1, 0)],
+    [(2, 0, 0), (-2, 0, 0), (0, 2, 0), (0, -2, 0)],
+    [(0, 4, 0), (0, -4, 0)],
+]
 
 
 def z_next(x):
@@ -109,33 +111,31 @@
 
 
 def unit_rows(t):
-    return slice(32, 40) if t == 3 else slice(8 * t, 8 * t + 8)
-
-
-def element_rows(t):
     return slice(8 * t, 8 * t + 8)
 
 
-def y_transform(ref, comp, plane, t):
-    a = ref[comp, plane, unit_rows(t), :]
-    if t < 3:
-        b = ref[comp, plane, 8 * t + 1 : 8 * t + 9, :]
-    else:
-        r = pltpu.roll(a, 7, 0)
-        b = jnp.where(rows_of() == 7, pltpu.roll(r, 128 - GROUP, 1), r)
-    return a + b, b - a
+def put_node(stores, ref, comp, plane, t, value):
+    follow = z_next(value)
+    first = 32 if t == 3 else 8 * t
+    for kind, x in enumerate((value + follow, follow - value)):
+        stores.append((ref, (kind, comp, plane, slice(first, first + 8)), x))
+        if t == 3:
+            stores.append((ref, (kind, comp, plane, slice(40, 48)), pltpu.roll(x, 128 - GROUP, 1)))
+
+
+def node_rows(ref, kind, comp, plane, t):
+    first = 32 if t == 3 else 8 * t
+    return ref[kind, comp, plane, first : first + 8, :], ref[kind, comp, plane, first + 1 : first + 9, :]
 
 
 def full_transform(ref, comp, plane, t):
-    s, d = y_transform(ref, comp, plane, t)
-    sn, dn = z_next(s), z_next(d)
-    return [s + sn, sn - s, d + dn, dn - d]
+    s, sn = node_rows(ref, 0, comp, plane, t)
+    d, dn = node_rows(ref, 1, comp, plane, t)
+    return [s + sn, d + dn, sn - s, dn - d]
 
 
 def central_transform(ref, comp, plane, t):
-    s, d = y_transform(ref, comp, plane, t)
-    sn, dn = z_next(s), z_next(d)
-    return [s + sn, sn - s, d + dn]
+    return full_transform(ref, comp, plane, t)[:3]
 
 
 def central_gradients(old, new):
@@ -169,13 +169,18 @@
     }
 
 
-def element_forces(modes):
+def element_forces(modes, modulus):
     first, shear = lame_pair()
     u, v, w = modes
-    s = stress_of([[m["DSS"], m["SDS"], m["SSD"]] for m in (u, v, w)])
-    sxx, syy, szz, syz, sxz, sxy = [x * (1.0 / 16.0) for x in s]
-    own, cross = (first + 3.0 * shear) / 48.0, first / 48.0
-    twist, cube = shear / 48.0, (first + 4.0 * shear) / 144.0
+    exx, eyy, ezz = u["DSS"], v["SDS"], w["SSD"]
+    normal, direct, slide = modulus * (first / 16.0), modulus * (shear / 8.0), modulus * (shear / 16.0)
+    base = normal * (exx + eyy + ezz)
+    sxx, syy, szz = base + direct * exx, base + direct * eyy, base + direct * ezz
+    syz = slide * (v["SSD"] + w["SDS"])
+    sxz = slide * (u["SSD"] + w["DSS"])
+    sxy = slide * (u["SDS"] + v["DSS"])
+    own, cross = modulus * ((first + 3.0 * shear) / 48.0), modulus * (first / 48.0)
+    twist, cube = modulus * (shear / 48.0), modulus * ((first + 4.0 * shear) / 144.0)
 
     def pair(a, b):
         return own * a + cross * b, cross * a + own * b
@@ -194,18 +199,24 @@
     ]
 
 
-def y_prev(value, kept, t):
-    r = pltpu.roll(value, 1, 0)
-    if t == 0:
-        return r, r
-    before = kept if t < 3 else pltpu.roll(r, GROUP, 1)
-    return jnp.where(rows_of() == 0, before, r), r
+def put_shifted(ref, index, t, value):
+    if t < 3:
+        ref[index, 8 * t + 1 : 8 * t + 9, :] = value
+    else:
+        ref[index, 33:41, :] = value
+        ref[index, 25:33, :] = pltpu.roll(value, GROUP, 1)
+
+
+def get_shifted(ref, index, t):
+    first = 32 if t == 3 else 8 * t
+    return ref[index, first : first + 8, :]
 
 
 def kernel(sizes, disp_in, dens_in, solid_in, mat_in, fixed_in, adj_out, sens_out,
            disp_v, dens_v, solid_v, mat_v, fixed_v, own, ylow, yhigh, zlow, zhigh, zlow_y, zhigh_y, yfirst,
-           rx, ry, rz, ryz, rxf, ryf, strip, tm, tn, fld, mod_e, grow, lead, rhs, v0, fv0, v1, fv1, adj, sens, merged,
-           carry_t, carry_p, src1, land1, src2, land2, in_sem, send_sem, recv_sem, s1, r1, s2, r2):
+           rx, ry, rz, ryz, rxf, ryf, strip, tm, tn, rows, fld, raw, mod_e, grow, lead, rhs, v0, fv0, v1, fv1, adj, fadj, sens,
+           merged, shifted,
+           carry_t, carry_p, src1, land1, src2, land2, in_sem, send_sem, recv_sem, s1, r1, s2, r2, known):
     position = [lax.axis_index(a) for a in AXES]
 
     def at(d):
@@ -223,7 +234,7 @@
     for copy in loads:
         copy.start()
     barrier = pltpu.get_barrier_semaphore()
-    greeted = GREETED + LATER + FIRST
+    greeted = LATER + FIRST
     for d in greeted:
         pl.semaphore_signal(barrier, inc=1, device_id=at(d), device_id_type=MESH)
     for copy in loads:
@@ -243,23 +254,29 @@
     lane16 = lax.broadcasted_iota(jnp.int32, (16, 128), 1)
     lane8 = lax.broadcasted_iota(jnp.int32, (8, 128), 1)
 
-    def pack_lanes(first_lane, ref, ref_y):
+    def pack_lanes(first_lane, offset, ref, ref_y):
         packed = jnp.zeros((16, 128), jnp.float32)
         for f in range(6):
             for p in range(BX):
-                group = 4 * (BX * f + p)
-                shift = (group - first_lane) % 128
+                place = 4 * (BX * f + p) + offset
+                shift = (place - first_lane) % 128
                 block = own[f, p]
-                packed = jnp.where(lane16 < group, packed, pltpu.roll(block, shift, 1) if shift else block)
+                packed = jnp.where(lane16 < place, packed, pltpu.roll(block, shift, 1) if shift else block)
         ref[...] = packed
         ref_y[0:4, :] = packed[0:4]
         ref_y[4:8, :] = packed[12:16]
 
-    pack_lanes(0, zlow, zlow_y)
+    pack_lanes(0, 0, zlow, zlow_y)
     for f in range(4):
         for p in range(BX):
             yfirst[BX * f + p : BX * f + p + 1, :] = own[f, p, 0:1, :]
 
+    pack_lanes(124, 4, zhigh, zhigh_y)
+    for f in range(6):
+        for p in range(BX):
+            half = 4 * (p % 2)
+            ylow[f, p // 2, half : half + 4, :] = own[f, p, 0:4, :]
+            yhigh[f, p // 2, half : half + 4, :] = own[f, p, 12:16, :]
     pl.semaphore_wait(barrier, len(greeted))
 
     def send(src, dst, d, sems, n, group):
@@ -280,15 +297,16 @@
             src, dst = (yfirst, ryf.at[sx - 1]) if dy else (own.at[pl.ds(0, 4), 0], rxf)
         send(src, dst, (dx, dy, dz), halo_sems, n, first)
 
-    pack_lanes(124, zhigh, zhigh_y)
-    for f in range(6):
-        for p in range(BX):
-            half = 4 * (p % 2)
-            ylow[f, p // 2, half : half + 4, :] = own[f, p, 0:4, :]
-            yhigh[f, p // 2, half : half + 4, :] = own[f, p, 12:16, :]
-    rest = [d for d in HALO if d not in FIRST or d[2] == 0]
-    rest.sort(key=lambda d: (d[2] != 0, d[1] != 0))
-    for n, (dx, dy, dz) in enumerate(rest):
+    def tell(n):
+        for d in ROUNDS[n]:
+            pl.semaphore_signal(known.at[n], inc=1, device_id=at(d), device_id_type=MESH)
+
+    def learn(n):
+        pl.semaphore_wait(known.at[n], len(ROUNDS[n]))
+
+    tell(0)
+    later_own = []
+    for n, (dx, dy, dz) in enumerate(REST):
         sx, sy, sz = 1 - dx, (1 - dy) // 2, (1 - dz) // 2
         if dz == 0 and dy == 0:
             src, dst = own, rx.at[sx // 2]
@@ -298,19 +316,24 @@
             src, dst = (zhigh if dz > 0 else zlow), rz.at[sx, sz]
         else:
             src, dst = (zhigh_y if dz > 0 else zlow_y), ryz.at[sx, sy, sz]
-        send(src, dst, (dx, dy, dz), halo_sems, len(FIRST) + n, later)
+        send(src, dst, (dx, dy, dz), halo_sems, len(FIRST) + n, later if dx else later_own)
+    learn(0)
+    tell(1)
 
     zero = jnp.zeros((8, 128), jnp.float32)
 
     def clear(p, _):
-        for f in range(6):
-            fld[f, p, 24:32, :] = zero
-        for c in range(3):
-            fv0[c, p, 24:32, :] = zero
-            fv1[c, p, 24:32, :] = zero
-            adj[c, p, 24:32, :] = zero
+        for kind in range(2):
+            for c in range(4):
+                fld[kind, c, p, 24:32, :] = zero
+            for c in range(3):
+                fv0[kind, c, p, 24:32, :] = zero
+                fv1[kind, c, p, 24:32, :] = zero
+                fadj[kind, c, p, 24:32, :] = zero
         return 0
 
+    for i in range(6):
+        shifted[i, 0:8, :] = zero
     lax.fori_loop(0, NP, clear, 0)
 
     def inside(axis, o):
@@ -357,59 +380,84 @@
             old = new
     src1[...] = partial
     sums1, sums2 = [], []
+    learn(1)
+    tell(2)
     for n, d in enumerate(plane):
         send(src1, land1.at[n], d, (s1, r1), n, sums1)
 
-    for copy in later:
-        copy.wait_recv()
-    for sx in range(3):
+    lane24 = lax.broadcasted_iota(jnp.int32, (24, 128), 1)
+    even_half = lane24 % 8 < 4
+    def merge_strips(sx):
+        sides = []
         for sz in range(2):
             f_xz = inside(0, sx - 1) * inside(2, 2 * sz - 1)
             strip[sx, sz, 0:4, :] = ryz[sx, 0, sz, 4:8, :] * (f_xz * inside(1, -1))
             strip[sx, sz, 4:20, :] = rz[sx, sz] * f_xz
             strip[sx, sz, 20:24, :] = ryz[sx, 1, sz, 0:4, :] * (f_xz * inside(1, 1))
+            sides.append(strip[sx, sz])
+        below, above = sides
+        strip[sx, 0] = jnp.where(even_half, above, below)
+        strip[sx, 1] = jnp.where(even_half, below, above)
 
     def flush(stores):
         for ref, index, value in stores:
             ref[index] = value
 
-    upper_half = rows_of() < 4
-
-    def unpack(f, _):
-        for sx in range(3):
+    def unpack(f, is_raw, parts):
+        for sx in parts:
             fx = inside(0, sx - 1)
+            for p in range(BX):
+                q = BX * sx + p
+                half = 4 * (p % 2)
+                rows[q, 4:20, :] = own[f, p] if sx == 1 else rx[sx // 2, f, p] * fx
+                rows[q, 0:4, :] = ry[sx, 0, f, p // 2, half : half + 4, :] * (fx * inside(1, -1))
+                rows[q, 20:24, :] = ry[sx, 1, f, p // 2, half : half + 4, :] * (fx * inside(1, 1))
+        for sx in parts:
             stores = []
             for p in range(BX):
                 q = BX * sx + p
-                a, b = [own[f, p, h : h + 8, :] if sx == 1 else rx[sx // 2, f, p, h : h + 8, :] * fx for h in (0, 8)]
-                a, b = pltpu.roll(a, 4, 0), pltpu.roll(b, 4, 0)
-                over, under = ry[sx, 0, f, p // 2] * (fx * inside(1, -1)), ry[sx, 1, f, p // 2] * (fx * inside(1, 1))
-                if p % 2:
-                    over = pltpu.roll(over, 4, 0)
-                else:
-                    under = pltpu.roll(under, 4, 0)
-                chunks = [jnp.where(upper_half, over, a), jnp.where(upper_half, a, b), jnp.where(upper_half, b, under)]
                 group = 4 * (BX * f + p)
-                ends = None
+                units, ends = [], None
                 for t in range(3):
                     base = GROUP * t
-                    below, above = strip[sx, 0, 8 * t : 8 * t + 8, :], strip[sx, 1, 8 * t : 8 * t + 8, :]
-                    value = jnp.where(lane8 < base + 12, pltpu.roll(above, lax.rem(base + 8 + 128 - group, 128), 1),
-                                      pltpu.roll(below, lax.rem(base + 12 + 128 - group, 128), 1))
-                    value = jnp.where(lane8 < base + 8, pltpu.roll(chunks[t], base + 8, 1), value)
-                    value = jnp.where(lane8 < base + 16, value, pltpu.roll(chunks[t], base + 16, 1))
+                    chunk = rows[q, 8 * t : 8 * t + 8, :]
+                    outer = strip[sx, p % 2, 8 * t : 8 * t + 8, :]
+                    value = jnp.where(lane8 < base + 16, pltpu.roll(outer, lax.rem(base + 8 + 128 - group, 128), 1),
+                                      pltpu.roll(chunk, base + 16, 1))
+                    value = jnp.where(lane8 < base + 8, pltpu.roll(chunk, base + 8, 1), value)
                     ends = value if ends is None else jnp.where(lane8 < base, ends, value)
-                    stores.append((fld, (f, q, slice(8 * t, 8 * t + 8)), chunks[t]))
-                stores.append((fld, (f, q, slice(32, 40)), ends))
+                    units.append(chunk)
+                units.append(ends)
+                for t, value in enumerate(units):
+                    if is_raw:
+                        stores.append((raw, (f - 4, q, unit_rows(t)), value))
+                    else:
+                        put_node(stores, fld, f, q, t, value)
             flush(stores)
-        return 0
-
-    lax.fori_loop(0, 6, unpack, 0)
+
+    def unpack_parts(copies, *parts):
+        for copy in copies:
+            copy.wait_recv()
+        for sx in parts:
+            merge_strips(sx)
+
+        def nodes(f, _):
+            unpack(f, False, parts)
+            return 0
+
+        def elements(f, _):
+            unpack(f, True, parts)
+            return 0
+
+        lax.fori_loop(0, 4, nodes, 0)
+        lax.fori_loop(4, 6, elements, 0)
+
+    unpack_parts(later_own, 1)
 
     kinds = ("SS", "SD", "DS", "DD")
 
-    def scatter(t, forces, kept, stores):
-        result, keep = [], []
+    def x_scatter(t, forces, stores):
+        result = []
         for c in range(3):
             by = {}
             for i, k in enumerate(kinds):
@@ -426,43 +474,55 @@
                     by[k] = carry_p[t, 4 * c + i] + (s - d)
                     upper = s + d
                 stores.append((carry_p, (t, 4 * c + i), upper))
-            rows = []
-            for k in ("S", "D"):
-                s, d = by[k + "S"], by.get(k + "D")
-                rows.append(s + z_prev(s) if d is None else (s - d) + z_prev(s + d))
-            down, r = y_prev(rows[0] + rows[1], None if kept is None else kept[c], t)
-            result.append((rows[0] - rows[1]) + down)
-            keep.append(r)
-        return result, keep
+            result.append(by)
+        return result
+
+    def yz_scatter(shares):
+        lower = []
+        for t, group in enumerate(shares):
+            for c, by in enumerate(group):
+                for i, k in enumerate("SD"):
+                    s, d = by["S" + k], by.get("D" + k)
+                    lower.append(s if d is None else s - d)
+                    put_shifted(shifted, 2 * c + i, t, s if d is None else s + d)
+        result = []
+        for t, group in enumerate(shares):
+            values = []
+            for c in range(len(group)):
+                s, d = [lower[6 * t + 2 * c + i] + get_shifted(shifted, 2 * c + i, t) for i in range(2)]
+                values.append((s - d) + z_prev(s + d))
+            result.append(values)
+        return result
 
     def clear_carry():
         for i in range(12):
             for t in range(UNITS):
                 carry_p[t, i] = zero
 
-    clear_carry()
-    for t in range(UNITS):
-        for c in range(3):
-            for i, value in enumerate(central_transform(fld, c, 0, t)):
-                carry_t[t, 4 * c + i] = value
-        s, _d = y_transform(fld, 3, 0, t)
-        carry_t[t, 12] = s + z_next(s)
+    def start_one(p):
+        clear_carry()
+        for t in range(UNITS):
+            for c in range(3):
+                for i, value in enumerate(central_transform(fld, c, p, t)):
+                    carry_t[t, 4 * c + i] = value
+            s, sn = node_rows(fld, 0, 3, p, t)
+            carry_t[t, 12] = s + sn
 
     def stage_one(e, _):
-        kept, stores = None, []
+        stores, shares = [], []
         first, shear = lame_pair()
         for t in range(UNITS):
-            nodes, cells = unit_rows(t), element_rows(t)
+            cells = unit_rows(t)
             grads = []
             for c in range(3):
                 new = central_transform(fld, c, e + 1, t)
                 old = [carry_t[t, 4 * c + i] for i in range(3)]
                 stores += [(carry_t, (t, 4 * c + i), value) for i, value in enumerate(new)]
                 grads.append([0.25 * g for g in central_gradients(old, new)])
-            s, _d = y_transform(fld, 3, e + 1, t)
-            mass = s + z_next(s)
+            s, sn = node_rows(fld, 0, 3, e + 1, t)
+            mass = s + sn
             rho = (carry_t[t, 12] + mass) * 0.125
-            rho_stiff = rho * rho * fld[5, e, nodes, :]
+            rho_stiff = rho * rho * raw[1, e, cells, :]
             modulus = rho_stiff * rho
             growth = 3.0 * rho_stiff
             stress = stress_of(grads)
@@ -484,20 +544,28 @@
             wzz = weight * (base + 2.0 * shear * hzz)
             skew = weight * (6.0 * shear)
             wyz, wxz, wxy = skew * syz, skew * sxz, skew * sxy
-            load, kept = scatter(t, [
+            shares.append(x_scatter(t, [
                 {"DSS": wxx, "SDS": wxy, "SSD": wxz},
                 {"DSS": wxy, "SDS": wyy, "SSD": wyz},
                 {"DSS": wxz, "SDS": wyz, "SSD": wzz},
-            ], kept, stores)
-            free = fld[4, e, nodes, :]
+            ], stores))
+        for t, load in enumerate(yz_scatter(shares)):
+            cells = unit_rows(t)
+            free = raw[0, e, cells, :]
             for c in range(3):
                 r = free * load[c]
                 d = r * (1.0 / theta)
-                stores += [(rhs, (c, e, nodes), r), (v0, (c, e, nodes), d), (fv0, (c, e, nodes), free * d)]
+                stores += [(rhs, (c, e, cells), r), (v0, (c, e, cells), d)]
+                put_node(stores, fv0, c, e, t, free * d)
         flush(stores)
         return 0
 
-    lax.fori_loop(0, NP - 1, stage_one, 0)
+    start_one(W)
+    lax.fori_loop(W, W + BX - 1, stage_one, 0)
+    unpack_parts(later, 0, 2)
+    lax.fori_loop(W + BX - 1, NP - 1, stage_one, 0)
+    start_one(0)
+    lax.fori_loop(0, W + 1, stage_one, 0)
 
     def apply_sweep(ref, first_plane, last_plane, node):
         clear_carry()
@@ -507,7 +575,7 @@
                     carry_t[t, 4 * c + i] = value
 
         def body(e, _):
-            kept, stores = None, []
+            stores, shares = [], []
             for t in range(UNITS):
                 modes = []
                 for c in range(3):
@@ -515,24 +583,24 @@
                     old = [carry_t[t, 4 * c + i] for i in range(4)]
                     stores += [(carry_t, (t, 4 * c + i), value) for i, value in enumerate(new)]
                     modes.append(element_modes(old, new))
-                modulus = mod_e[e, element_rows(t), :]
-                forces = [{k: modulus * f for k, f in g.items()} for g in element_forces(modes)]
-                applied, kept = scatter(t, forces, kept, stores)
-                free = fld[4, e, unit_rows(t), :]
+                forces = element_forces(modes, mod_e[e, unit_rows(t), :])
+                shares.append(x_scatter(t, forces, stores))
+            for t, applied in enumerate(yz_scatter(shares)):
+                free = raw[0, e, unit_rows(t), :]
                 for c in range(3):
-                    node(c, e, unit_rows(t), free, applied[c], stores)
+                    node(c, e, t, free, applied[c], stores)
             flush(stores)
             return 0
 
         lax.fori_loop(first_plane, last_plane, body, 0)
 
-    def node_two(c, e, rows, free, applied, stores):
-        d = v0[c, e, rows, :]
-        r = rhs[c, e, rows, :] - (free * applied + (1.0 - free) * d)
+    def node_two(c, e, t, free, applied, stores):
+        cells = unit_rows(t)
+        d = v0[c, e, cells, :]
+        r = rhs[c, e, cells, :] - (free * applied + (1.0 - free) * d)
         new = (rho_one * rho_zero) * d + (2.0 * rho_one / delta) * r
-        stores += [(rhs, (c, e, rows), r), (v1, (c, e, rows), new), (fv1, (c, e, rows), free * new)]
-
-    apply_sweep(fv0, 1, NP - 2, node_two)
+        stores += [(rhs, (c, e, cells), r), (v1, (c, e, cells), new)]
+        put_node(stores, fv1, c, e, t, free * new)
 
     for copy in sums1:
         copy.wait_recv()
@@ -540,46 +608,55 @@
     for n in range(len(plane)):
         total = total + land1[n]
     src2[...] = total
+    learn(2)
     for n, d in enumerate(ring):
         send(src2, land2.at[n], d, (s2, r2), n, sums2)
 
-    def node_three(c, e, rows, free, applied, stores):
-        d = v1[c, e, rows, :]
-        r = rhs[c, e, rows, :] - (free * applied + (1.0 - free) * d)
+    apply_sweep(fv0, 1, NP - 2, node_two)
+
+    def node_three(c, e, t, free, applied, stores):
+        cells = unit_rows(t)
+        d = v1[c, e, cells, :]
+        r = rhs[c, e, cells, :] - (free * applied + (1.0 - free) * d)
         new = (rho_two * rho_one) * d + (2.0 * rho_two / delta) * r
-        stores.append((adj, (c, e, rows), v0[c, e, rows, :] + d + new))
+        value = v0[c, e, cells, :] + d + new
+        stores.append((adj, (c, e, cells), value))
+        put_node(stores, fadj, c, e, t, value)
 
     apply_sweep(fv1, 2, NP - 3, node_three)
 
     for t in range(UNITS):
         carry_p[t, 0] = zero
         for c in range(3):
-            for i, value in enumerate(full_transform(adj, c, W - 1, t)):
+            for i, value in enumerate(full_transform(fadj, c, W - 1, t)):
                 carry_t[t, 4 * c + i] = value
             for i, value in enumerate(full_transform(fld, c, W - 1, t)):
                 carry_t[t, 12 + 4 * c + i] = value
 
     def stage_four(e, _):
-        kept, stores = None, []
+        stores, shares = [], []
         for t in range(UNITS):
             modes = []
-            for ref, base in ((fld, 12), (adj, 0)):
+            for ref, base in ((fld, 12), (fadj, 0)):
                 group = []
                 for c in range(3):
                     new = full_transform(ref, c, e + 1, t)
                     old = [carry_t[t, base + 4 * c + i] for i in range(4)]
                     stores += [(carry_t, (t, base + 4 * c + i), value) for i, value in enumerate(new)]
                     group.append(element_modes(old, new))
-                modes.append(group if ref is adj else element_forces(group))
+                modes.append(group if base == 0 else element_forces(group, 1.0))
             work = None
             for f, a in zip(*modes):
                 for k, value in f.items():
                     work = a[k] * value if work is None else work + a[k] * value
-            g = lead[e, element_rows(t), :] - grow[e, element_rows(t), :] * work
+            g = lead[e, unit_rows(t), :] - grow[e, unit_rows(t), :] * work
             share = g + carry_p[t, 0]
-            share = share + z_prev(share)
-            down, kept = y_prev(share, kept, t)
-            stores += [(carry_p, (t, 0), g), (sens, (e, element_rows(t)), share + down)]
+            stores.append((carry_p, (t, 0), g))
+            put_shifted(shifted, 0, t, share)
+            shares.append(share)
+        for t, share in enumerate(shares):
+            share = share + get_shifted(shifted, 0, t)
+            stores.append((sens, (e, unit_rows(t)), share + z_prev(share)))
         flush(stores)
         return 0
 
@@ -587,7 +664,7 @@
 
     for c in range(4):
         for p in range(BX):
-            main, ends = ((sens.at[W + p], sens[W + p, 24:32, :]) if c == 3 else (adj.at[c, W + p], adj[c, W + p, 32:40, :]))
+            main, ends = ((sens.at[W + p], sens[W + p, 24:32, :]) if c == 3 else (adj.at[c, W + p], adj[c, W + p, 24:32, :]))
             for t in range(3):
                 base = GROUP * t
                 value = jnp.where(lane8 < 4, pltpu.roll(ends, (128 - 16 - base) % 128, 1), main[8 * t : 8 * t + 8, :])
@@ -595,6 +672,8 @@
                     lane8 >= 124, pltpu.roll(ends, (120 - base) % 128, 1), value
                 )
 
+    for copy in first + later_own + later + sums1:
+        copy.wait_send()
     for copy in sums2:
         copy.wait_recv()
     total = src2[...]
@@ -611,7 +690,7 @@
             for c in range(3):
                 adj_out[c, p, h : h + 8, :] = scale * merged[c, p, h + 4 : h + 12, :]
 
-    for copy in first + later + sums1 + sums2:
+    for copy in sums2:
         copy.wait_send()
 
 
@@ -628,7 +707,7 @@
     f32, i32 = jnp.float32, jnp.int32
     vm = pltpu.VMEM
     dma = pltpu.SemaphoreType.DMA
-    node = (3, NP, ROWS, 128)
+    node, paired = (3, NP, 32, 128), (2, 3, NP, ROWS, 128)
     element = (NP, 32, 128)
     tile = (8, 128)
     messages = len(HALO) + 3
@@ -639,14 +718,15 @@
         vm((2, 6, BX, BY, BZ), f32), vm((3, 2, 6, 2, 8, 128), f32), vm((3, 2, 16, 128), f32), vm((3, 2, 2, 8, 128), f32),
         vm((4, 16, 128), f32), vm((2, 16, 128), f32),
         vm((3, 2, 24, 128), f32), vm((4, BX + 1, 24, 128), f32), vm((4, BX + 1, 24, 128), f32),
-        vm((6, NP, ROWS, 128), f32),
+        vm((NP, 24, 128), f32), vm((2, 4, NP, ROWS, 128), f32), vm((2, NP, 32, 128), f32),
         vm(element, f32), vm(element, f32), vm(element, f32),
-        vm(node, f32), vm(node, f32), vm(node, f32), vm(node, f32), vm(node, f32), vm(node, f32),
-        vm(element, f32), vm((4, BX, 24, 128), f32),
+        vm(node, f32), vm(node, f32), vm(paired, f32), vm(node, f32), vm(paired, f32), vm(node, f32), vm(paired, f32),
+        vm(element, f32), vm((4, BX, 24, 128), f32), vm((6, ROWS, 128), f32),
         vm((UNITS, 24, 8, 128), f32), vm((UNITS, 12, 8, 128), f32),
         vm(tile, f32), vm((len(plane), 8, 128), f32), vm(tile, f32), vm((len(ring), 8, 128), f32),
         dma((5,)), dma((messages,)), dma((messages,)),
         dma((len(plane),)), dma((len(plane),)), dma((len(ring),)), dma((len(ring),)),
+        pltpu.SemaphoreType.REGULAR((len(ROUNDS),)),
     ]
     outs = (jax.ShapeDtypeStruct((3, BX, BY, BZ), f32), jax.ShapeDtypeStruct((BX, BY, BZ), f32))
     results = pl.pallas_call(

time: 42.3 us -> 36.1 us (0.85); the launches traced: 42.2 us -> 35.5 us
  Pallas kernels: 41.5 us -> 34.8 us
    pallas_call x1, Pallas kernels: 40.9 us -> 34.2 us  [local(): pl.pallas_call(functools.partial(kernel, sizes), out_shape=outs, in_specs...]
where the time goes in v2:
time: 36.1 us; the launch traced here: 35.5 us
  Pallas kernels  34.8 us (96%)
  between operations  0.64 us (2%)
    pallas_call x1, Pallas kernels, local(): pl.pallas_call(functools.partial(kernel, sizes), out_shape=outs, in_specs...  34.2 us

profile of v2, /device:TPU:1, one launch (start us, length us, event | category | flops | bytes accessed | tf_op | source)
XLA Modules:
  0.0 35.5 jit_solution(15491314647975786854)
XLA Ops:
  0.6 34.2 %shard_map.68 = (f32[3,4,16,128]{3,2,1,0:T(8,128)S(1)}, f32[4,16,128]{2,1,0:T(8,128)S(1)}) custom-call(f32[3,4,16,128]{3,2,1,0:T(8,128)} %disp_in.1, f32[4,16,128]{2,1,0:T(8,128)} %dens_in.1, s32[4,16,128]{2,1,0:T(8,128)} %solid_in.1, s32[4,16,128]{2,1,0:T(8,128)} %mat_in.1, s32[4,16,128]{2,1,0:T(8,128)} %fixed_in.1), custom_call_target="tpu_custom_call" | custom-call | tf_op jit(solution)/shard_map/pallas_call | solution.py:732
  34.8 0.7 %shard_map.69 = (f32[3,4,16,128]{3,2,1,0:T(8,128)}, f32[4,16,128]{2,1,0:T(8,128)}) custom-call(f32[3,4,16,128]{3,2,1,0:T(8,128)S(1)} %get-tuple-element.4.adj_in, f32[4,16,128]{2,1,0:T(8,128)S(1)} %get-tuple-element.5.sens_in), custom_call_target="tpu_custom_call" | custom-call | tf_op jit(solution)/shard_map/pallas_call | solution.py:742

commit v3 on v2

--- a/solution.py
+++ b/solution.py
@@ -18,7 +18,7 @@
 BX, BY, BZ = 4, 16, 128
 W = 4
 NP = BX + 2 * W
-ROWS = 48
+ROWS = 56
 UNITS = 4
 GROUP = 24
 
@@ -118,14 +118,14 @@
     follow = z_next(value)
     first = 32 if t == 3 else 8 * t
     for kind, x in enumerate((value + follow, follow - value)):
-        stores.append((ref, (kind, comp, plane, slice(first, first + 8)), x))
+        stores.append((ref, (plane, kind, comp, slice(first, first + 8)), x))
         if t == 3:
-            stores.append((ref, (kind, comp, plane, slice(40, 48)), pltpu.roll(x, 128 - GROUP, 1)))
+            stores.append((ref, (plane, kind, comp, slice(40, 48)), pltpu.roll(x, 128 - GROUP, 1)))
 
 
 def node_rows(ref, kind, comp, plane, t):
     first = 32 if t == 3 else 8 * t
-    return ref[kind, comp, plane, first : first + 8, :], ref[kind, comp, plane, first + 1 : first + 9, :]
+    return ref[plane, kind, comp, first : first + 8, :], ref[plane, kind, comp, first + 1 : first + 9, :]
 
 
 def full_transform(ref, comp, plane, t):
@@ -215,7 +215,7 @@
 def kernel(sizes, disp_in, dens_in, solid_in, mat_in, fixed_in, adj_out, sens_out,
            disp_v, dens_v, solid_v, mat_v, fixed_v, own, ylow, yhigh, zlow, zhigh, zlow_y, zhigh_y, yfirst,
            rx, ry, rz, ryz, rxf, ryf, strip, tm, tn, rows, fld, raw, mod_e, grow, lead, rhs, v0, fv0, v1, fv1, adj, fadj, sens,
-           merged, shifted,
+           merged, shifted, lowers,
            carry_t, carry_p, src1, land1, src2, land2, in_sem, send_sem, recv_sem, s1, r1, s2, r2, known):
     position = [lax.axis_index(a) for a in AXES]
 
@@ -304,7 +304,6 @@
     def learn(n):
         pl.semaphore_wait(known.at[n], len(ROUNDS[n]))
 
-    tell(0)
     later_own = []
     for n, (dx, dy, dz) in enumerate(REST):
         sx, sy, sz = 1 - dx, (1 - dy) // 2, (1 - dz) // 2
@@ -317,6 +316,8 @@
         else:
             src, dst = (zhigh_y if dz > 0 else zlow_y), ryz.at[sx, sy, sz]
         send(src, dst, (dx, dy, dz), halo_sems, len(FIRST) + n, later if dx else later_own)
+        if n == 7:
+            tell(0)
     learn(0)
     tell(1)
 
@@ -325,15 +326,18 @@
     def clear(p, _):
         for kind in range(2):
             for c in range(4):
-                fld[kind, c, p, 24:32, :] = zero
+                fld[p, kind, c, 24:32, :] = zero
             for c in range(3):
-                fv0[kind, c, p, 24:32, :] = zero
-                fv1[kind, c, p, 24:32, :] = zero
-                fadj[kind, c, p, 24:32, :] = zero
+                fv0[p, kind, c, 24:32, :] = zero
+                fv1[p, kind, c, 24:32, :] = zero
+                fadj[p, kind, c, 24:32, :] = zero
         return 0
 
     for i in range(6):
         shifted[i, 0:8, :] = zero
+    for i in range(24):
+        lowers[i] = zero
+        shifted[i % 6, 8 + 8 * (i // 6) : 16 + 8 * (i // 6), :] = zero
     lax.fori_loop(0, NP, clear, 0)
 
     def inside(axis, o):
@@ -430,7 +434,7 @@
                 units.append(ends)
                 for t, value in enumerate(units):
                     if is_raw:
-                        stores.append((raw, (f - 4, q, unit_rows(t)), value))
+                        stores.append((raw, (q, f - 4, unit_rows(t)), value))
                     else:
                         put_node(stores, fld, f, q, t, value)
             flush(stores)
@@ -477,19 +481,26 @@
             result.append(by)
         return result
 
-    def yz_scatter(shares):
-        lower = []
+    def leave(shares, stores):
         for t, group in enumerate(shares):
             for c, by in enumerate(group):
                 for i, k in enumerate("SD"):
                     s, d = by["S" + k], by.get("D" + k)
-                    lower.append(s if d is None else s - d)
-                    put_shifted(shifted, 2 * c + i, t, s if d is None else s + d)
+                    lower, upper = (s, s) if d is None else (s - d, s + d)
+                    stores.append((lowers, 6 * t + 2 * c + i, lower))
+                    index = 2 * c + i
+                    if t < 3:
+                        stores.append((shifted, (index, slice(8 * t + 1, 8 * t + 9)), upper))
+                    else:
+                        stores.append((shifted, (index, slice(33, 41)), upper))
+                        stores.append((shifted, (index, slice(25, 33)), pltpu.roll(upper, GROUP, 1)))
+
+    def take_up():
         result = []
-        for t, group in enumerate(shares):
+        for t in range(UNITS):
             values = []
-            for c in range(len(group)):
-                s, d = [lower[6 * t + 2 * c + i] + get_shifted(shifted, 2 * c + i, t) for i in range(2)]
+            for c in range(3):
+                s, d = [lowers[6 * t + 2 * c + i] + get_shifted(shifted, 2 * c + i, t) for i in range(2)]
                 values.append((s - d) + z_prev(s + d))
             result.append(values)
         return result
@@ -508,8 +519,19 @@
             s, sn = node_rows(fld, 0, 3, p, t)
             carry_t[t, 12] = s + sn
 
+    def nodes_one(e, stores):
+        for t, load in enumerate(take_up()):
+            cells = unit_rows(t)
+            free = raw[e, 0, cells, :]
+            for c in range(3):
+                r = free * load[c]
+                d = r * (1.0 / theta)
+                stores += [(rhs, (e, c, cells), r), (v0, (e, c, cells), d)]
+                put_node(stores, fv0, c, e, t, free * d)
+
     def stage_one(e, _):
         stores, shares = [], []
+        nodes_one(jnp.maximum(e - 1, 0), stores)
         first, shear = lame_pair()
         for t in range(UNITS):
             cells = unit_rows(t)
@@ -522,7 +544,7 @@
             s, sn = node_rows(fld, 0, 3, e + 1, t)
             mass = s + sn
             rho = (carry_t[t, 12] + mass) * 0.125
-            rho_stiff = rho * rho * raw[1, e, cells, :]
+            rho_stiff = rho * rho * raw[e, 1, cells, :]
             modulus = rho_stiff * rho
             growth = 3.0 * rho_stiff
             stress = stress_of(grads)
@@ -549,23 +571,34 @@
                 {"DSS": wxy, "SDS": wyy, "SSD": wyz},
                 {"DSS": wxz, "SDS": wyz, "SSD": wzz},
             ], stores))
-        for t, load in enumerate(yz_scatter(shares)):
-            cells = unit_rows(t)
-            free = raw[0, e, cells, :]
-            for c in range(3):
-                r = free * load[c]
-                d = r * (1.0 / theta)
-                stores += [(rhs, (c, e, cells), r), (v0, (c, e, cells), d)]
-                put_node(stores, fv0, c, e, t, free * d)
+        leave(shares, stores)
         flush(stores)
         return 0
 
+    def sweep_one(low, high):
+        lax.fori_loop(low, high, stage_one, 0)
+        stores = []
+        nodes_one(high - 1, stores)
+        flush(stores)
+
     start_one(W)
-    lax.fori_loop(W, W + BX - 1, stage_one, 0)
+    sweep_one(W, W + BX - 1)
+    for copy in first + later_own + later:
+        copy.wait_send()
     unpack_parts(later, 0, 2)
-    lax.fori_loop(W + BX - 1, NP - 1, stage_one, 0)
+    sweep_one(W + BX - 1, NP - 1)
+    for copy in sums1:
+        copy.wait_recv()
+    total = src1[...]
+    for n in range(len(plane)):
+        total = total + land1[n]
+    src2[...] = total
+    learn(2)
+    for n, d in enumerate(ring):
+        send(src2, land2.at[n], d, (s2, r2), n, sums2)
+
     start_one(0)
-    lax.fori_loop(0, W + 1, stage_one, 0)
+    sweep_one(0, W + 1)
 
     def apply_sweep(ref, first_plane, last_plane, node):
         clear_carry()
@@ -574,8 +607,15 @@
                 for i, value in enumerate(full_transform(ref, c, first_plane, t)):
                     carry_t[t, 4 * c + i] = value
 
+        def nodes(e, stores):
+            for t, applied in enumerate(take_up()):
+                free = raw[e, 0, unit_rows(t), :]
+                for c in range(3):
+                    node(c, e, t, free, applied[c], stores)
+
         def body(e, _):
             stores, shares = [], []
+            nodes(e - 1, stores)
             for t in range(UNITS):
                 modes = []
                 for c in range(3):
@@ -585,42 +625,32 @@
                     modes.append(element_modes(old, new))
                 forces = element_forces(modes, mod_e[e, unit_rows(t), :])
                 shares.append(x_scatter(t, forces, stores))
-            for t, applied in enumerate(yz_scatter(shares)):
-                free = raw[0, e, unit_rows(t), :]
-                for c in range(3):
-                    node(c, e, t, free, applied[c], stores)
+            leave(shares, stores)
             flush(stores)
             return 0
 
         lax.fori_loop(first_plane, last_plane, body, 0)
+        stores = []
+        nodes(last_plane - 1, stores)
+        flush(stores)
 
     def node_two(c, e, t, free, applied, stores):
         cells = unit_rows(t)
-        d = v0[c, e, cells, :]
-        r = rhs[c, e, cells, :] - (free * applied + (1.0 - free) * d)
+        d = v0[e, c, cells, :]
+        r = rhs[e, c, cells, :] - (free * applied + (1.0 - free) * d)
         new = (rho_one * rho_zero) * d + (2.0 * rho_one / delta) * r
-        stores += [(rhs, (c, e, cells), r), (v1, (c, e, cells), new)]
+        stores += [(rhs, (e, c, cells), r), (v1, (e, c, cells), new)]
         put_node(stores, fv1, c, e, t, free * new)
-
-    for copy in sums1:
-        copy.wait_recv()
-    total = src1[...]
-    for n in range(len(plane)):
-        total = total + land1[n]
-    src2[...] = total
-    learn(2)
-    for n, d in enumerate(ring):
-        send(src2, land2.at[n], d, (s2, r2), n, sums2)
 
     apply_sweep(fv0, 1, NP - 2, node_two)
 
     def node_three(c, e, t, free, applied, stores):
         cells = unit_rows(t)
-        d = v1[c, e, cells, :]
-        r = rhs[c, e, cells, :] - (free * applied + (1.0 - free) * d)
+        d = v1[e, c, cells, :]
+        r = rhs[e, c, cells, :] - (free * applied + (1.0 - free) * d)
         new = (rho_two * rho_one) * d + (2.0 * rho_two / delta) * r
-        value = v0[c, e, cells, :] + d + new
-        stores.append((adj, (c, e, cells), value))
+        value = v0[e, c, cells, :] + d + new
+        stores.append((adj, (e, c, cells), value))
         put_node(stores, fadj, c, e, t, value)
 
     apply_sweep(fv1, 2, NP - 3, node_three)
@@ -664,7 +694,7 @@
 
     for c in range(4):
         for p in range(BX):
-            main, ends = ((sens.at[W + p], sens[W + p, 24:32, :]) if c == 3 else (adj.at[c, W + p], adj[c, W + p, 24:32, :]))
+            main, ends = ((sens.at[W + p], sens[W + p, 24:32, :]) if c == 3 else (adj.at[W + p, c], adj[W + p, c, 24:32, :]))
             for t in range(3):
                 base = GROUP * t
                 value = jnp.where(lane8 < 4, pltpu.roll(ends, (128 - 16 - base) % 128, 1), main[8 * t : 8 * t + 8, :])
@@ -672,7 +702,7 @@
                     lane8 >= 124, pltpu.roll(ends, (120 - base) % 128, 1), value
                 )
 
-    for copy in first + later_own + later + sums1:
+    for copy in sums1:
         copy.wait_send()
     for copy in sums2:
         copy.wait_recv()
@@ -707,7 +737,7 @@
     f32, i32 = jnp.float32, jnp.int32
     vm = pltpu.VMEM
     dma = pltpu.SemaphoreType.DMA
-    node, paired = (3, NP, 32, 128), (2, 3, NP, ROWS, 128)
+    node, paired = (NP, 3, 40, 128), (NP, 2, 3, ROWS, 128)
     element = (NP, 32, 128)
     tile = (8, 128)
     messages = len(HALO) + 3
@@ -718,10 +748,10 @@
         vm((2, 6, BX, BY, BZ), f32), vm((3, 2, 6, 2, 8, 128), f32), vm((3, 2, 16, 128), f32), vm((3, 2, 2, 8, 128), f32),
         vm((4, 16, 128), f32), vm((2, 16, 128), f32),
         vm((3, 2, 24, 128), f32), vm((4, BX + 1, 24, 128), f32), vm((4, BX + 1, 24, 128), f32),
-        vm((NP, 24, 128), f32), vm((2, 4, NP, ROWS, 128), f32), vm((2, NP, 32, 128), f32),
+        vm((NP, 24, 128), f32), vm((NP, 2, 4, ROWS, 128), f32), vm((NP, 2, 40, 128), f32),
         vm(element, f32), vm(element, f32), vm(element, f32),
         vm(node, f32), vm(node, f32), vm(paired, f32), vm(node, f32), vm(paired, f32), vm(node, f32), vm(paired, f32),
-        vm(element, f32), vm((4, BX, 24, 128), f32), vm((6, ROWS, 128), f32),
+        vm(element, f32), vm((4, BX, 24, 128), f32), vm((6, ROWS, 128), f32), vm((24, 8, 128), f32),
         vm((UNITS, 24, 8, 128), f32), vm((UNITS, 12, 8, 128), f32),
         vm(tile, f32), vm((len(plane), 8, 128), f32), vm(tile, f32), vm((len(ring), 8, 128), f32),
         dma((5,)), dma((messages,)), dma((messages,)),

time: 36.1 us -> 34.2 us (0.947); the launches traced: 35.5 us -> 34 us
  Pallas kernels: 34.8 us -> 33.3 us
    pallas_call x1, Pallas kernels: 34.2 us -> 32.7 us  [local(): pl.pallas_call(functools.partial(kernel, sizes), out_shape=outs, in_specs...]
where the time goes in v3:
time: 34.2 us; the launch traced here: 34 us
  Pallas kernels  33.3 us (97%)
  between operations  0.64 us (2%)
    pallas_call x1, Pallas kernels, local(): pl.pallas_call(functools.partial(kernel, sizes), out_shape=outs, in_specs...  32.7 us

profile of v3, /device:TPU:1, one launch (start us, length us, event | category | flops | bytes accessed | tf_op | source)
XLA Modules:
  0.0 34.0 jit_solution(5548654232361211251)
XLA Ops:
  0.6 32.7 %shard_map.68 = (f32[3,4,16,128]{3,2,1,0:T(8,128)S(1)}, f32[4,16,128]{2,1,0:T(8,128)S(1)}) custom-call(f32[3,4,16,128]{3,2,1,0:T(8,128)} %disp_in.1, f32[4,16,128]{2,1,0:T(8,128)} %dens_in.1, s32[4,16,128]{2,1,0:T(8,128)} %solid_in.1, s32[4,16,128]{2,1,0:T(8,128)} %mat_in.1, s32[4,16,128]{2,1,0:T(8,128)} %fixed_in.1), custom_call_target="tpu_custom_call" | custom-call | tf_op jit(solution)/shard_map/pallas_call | solution.py:762
  33.3 0.7 %shard_map.69 = (f32[3,4,16,128]{3,2,1,0:T(8,128)}, f32[4,16,128]{2,1,0:T(8,128)}) custom-call(f32[3,4,16,128]{3,2,1,0:T(8,128)S(1)} %get-tuple-element.4.adj_in, f32[4,16,128]{2,1,0:T(8,128)S(1)} %get-tuple-element.5.sens_in), custom_call_target="tpu_custom_call" | custom-call | tf_op jit(solution)/shard_map/pallas_call | solution.py:772

commit v4 on v3

--- a/solution.py
+++ b/solution.py
@@ -527,10 +527,17 @@
                 r = free * load[c]
                 d = r * (1.0 / theta)
                 stores += [(rhs, (e, c, cells), r), (v0, (e, c, cells), d)]
-                put_node(stores, fv0, c, e, t, free * d)
+
+    def pair_up(source, made, e, stores, masked=True):
+        for t in range(UNITS):
+            free = raw[e, 0, unit_rows(t), :]
+            for c in range(3):
+                value = source[e, c, unit_rows(t), :]
+                put_node(stores, made, c, e, t, free * value if masked else value)
 
     def stage_one(e, _):
         stores, shares = [], []
+        pair_up(v0, fv0, jnp.maximum(e - 2, 0), stores)
         nodes_one(jnp.maximum(e - 1, 0), stores)
         first, shear = lame_pair()
         for t in range(UNITS):
@@ -578,7 +585,11 @@
     def sweep_one(low, high):
         lax.fori_loop(low, high, stage_one, 0)
         stores = []
+        pair_up(v0, fv0, high - 2, stores)
         nodes_one(high - 1, stores)
+        flush(stores)
+        stores = []
+        pair_up(v0, fv0, high - 1, stores)
         flush(stores)
 
     start_one(W)
@@ -600,7 +611,7 @@
     start_one(0)
     sweep_one(0, W + 1)
 
-    def apply_sweep(ref, first_plane, last_plane, node):
+    def apply_sweep(ref, first_plane, last_plane, node, source, made, masked):
         clear_carry()
         for t in range(UNITS):
             for c in range(3):
@@ -615,6 +626,7 @@
 
         def body(e, _):
             stores, shares = [], []
+            pair_up(source, made, jnp.maximum(e - 2, 0), stores, masked)
             nodes(e - 1, stores)
             for t in range(UNITS):
                 modes = []
@@ -631,7 +643,11 @@
 
         lax.fori_loop(first_plane, last_plane, body, 0)
         stores = []
+        pair_up(source, made, last_plane - 2, stores, masked)
         nodes(last_plane - 1, stores)
+        flush(stores)
+        stores = []
+        pair_up(source, made, last_plane - 1, stores, masked)
         flush(stores)
 
     def node_two(c, e, t, free, applied, stores):
@@ -640,9 +656,8 @@
         r = rhs[e, c, cells, :] - (free * applied + (1.0 - free) * d)
         new = (rho_one * rho_zero) * d + (2.0 * rho_one / delta) * r
         stores += [(rhs, (e, c, cells), r), (v1, (e, c, cells), new)]
-        put_node(stores, fv1, c, e, t, free * new)
-
-    apply_sweep(fv0, 1, NP - 2, node_two)
+
+    apply_sweep(fv0, 1, NP - 2, node_two, v1, fv1, True)
 
     def node_three(c, e, t, free, applied, stores):
         cells = unit_rows(t)
@@ -651,9 +666,8 @@
         new = (rho_two * rho_one) * d + (2.0 * rho_two / delta) * r
         value = v0[e, c, cells, :] + d + new
         stores.append((adj, (e, c, cells), value))
-        put_node(stores, fadj, c, e, t, value)
-
-    apply_sweep(fv1, 2, NP - 3, node_three)
+
+    apply_sweep(fv1, 2, NP - 3, node_three, adj, fadj, False)
 
     for t in range(UNITS):
         carry_p[t, 0] = zero

time: 34.2 us -> 33.9 us (level)
  Pallas kernels: 33.3 us -> 32.7 us
    pallas_call x1, Pallas kernels: 32.7 us -> 32.1 us  [local(): pl.pallas_call(functools.partial(kernel, sizes), out_shape=outs, in_specs...]
where the time goes in v4:
time: 33.9 us; the launch traced here: 33.4 us
  Pallas kernels  32.7 us (96%)
  between operations  0.64 us (2%)
    pallas_call x1, Pallas kernels, local(): pl.pallas_call(functools.partial(kernel, sizes), out_shape=outs, in_specs...  32.1 us

profile of v4, /device:TPU:1, one launch (start us, length us, event | category | flops | bytes accessed | tf_op | source)
XLA Modules:
  0.0 33.4 jit_solution(11594327108402310103)
XLA Ops:
  0.6 32.1 %shard_map.68 = (f32[3,4,16,128]{3,2,1,0:T(8,128)S(1)}, f32[4,16,128]{2,1,0:T(8,128)S(1)}) custom-call(f32[3,4,16,128]{3,2,1,0:T(8,128)} %disp_in.1, f32[4,16,128]{2,1,0:T(8,128)} %dens_in.1, s32[4,16,128]{2,1,0:T(8,128)} %solid_in.1, s32[4,16,128]{2,1,0:T(8,128)} %mat_in.1, s32[4,16,128]{2,1,0:T(8,128)} %fixed_in.1), custom_call_target="tpu_custom_call" | custom-call | tf_op jit(solution)/shard_map/pallas_call | solution.py:776
  32.7 0.7 %shard_map.69 = (f32[3,4,16,128]{3,2,1,0:T(8,128)}, f32[4,16,128]{2,1,0:T(8,128)}) custom-call(f32[3,4,16,128]{3,2,1,0:T(8,128)S(1)} %get-tuple-element.4.adj_in, f32[4,16,128]{2,1,0:T(8,128)S(1)} %get-tuple-element.5.sens_in), custom_call_target="tpu_custom_call" | custom-call | tf_op jit(solution)/shard_map/pallas_call | solution.py:786
